TPU v7x, 128 devices: a whole 4x4x4 slice. The times are simulated.
128 devices in a mesh: basis: 8 (over y, x_hi), aux: 16 (over x_lo, z, core).
Axes of the slice: x: 4 (x_hi: 2, x_lo: 2; x = x_hi * 2 + x_lo), y: 4, z: 4, core: 2. Of those that a mesh axis runs over, the one named last changes fastest.
Arguments:
- half_ints: bfloat16 [2, 8000, 24000], P(None, 'basis', 'aux'), may hold values from -6 to 6
- virt_coeffs: bfloat16 [8000, 768], P('basis'), may hold values from -0.0625 to 0.0625
- metric_factor: bfloat16 [24000, 24000], P('aux', 'basis'), as said below
Outputs:
- fitted: float32 [1536, 24000], P('aux', 'basis')
Inputs may be any that keep to these rules, and one draw needn't show every extreme that they name: metric_factor is zero where the row index exceeds the column index; its diagonal is positive.
All inputs are finite; a program needn't handle non-finite values.
Results may differ from a plain program's by a relative error of at most 0.0029.
Values may be sent and summed in bfloat16 or wider, within the bound.
No kernel may reach another device: no remote copies, remote signals or barrier semaphores. Data moves between devices by JAX's collectives and lax.ppermute only.
A program may use at most 128 MiB of HBM per device.

v0:
```python
import jax
import jax.numpy as jnp
from jax import lax
from jax.sharding import PartitionSpec as P


def orbital_block(virt_coeffs, slab):
    return lax.dot_general(
        virt_coeffs, slab, (((0,), (0,)), ((), ())), preferred_element_type=jnp.float32
    )


def metric_apply(rows_all, metric_factor):
    return jnp.dot(rows_all, metric_factor, preferred_element_type=jnp.float32)


def on_device(half_ints, virt_coeffs, metric_factor):
    n_occ = half_ints.shape[0]
    n_vir = virt_coeffs.shape[1]
    width = half_ints.shape[2]
    blocks = []
    for occ in range(n_occ):
        blocks.append(orbital_block(virt_coeffs, half_ints[occ]))
    partial_ints = jnp.stack(blocks, axis=1).reshape(n_vir * n_occ, width)
    pair_ints = lax.psum(partial_ints, "basis").astype(jnp.bfloat16)
    fitted = lax.psum_scatter(
        metric_apply(pair_ints, metric_factor), "aux", scatter_dimension=0, tiled=True
    )
    return fitted


def solution(mesh):
    placed = (P(None, "basis", "aux"), P("basis", None), P("aux", "basis"))
    return jax.shard_map(
        on_device, mesh=mesh, in_specs=placed, out_specs=P("aux", "basis"), check_vma=False
    )
```

profile of v0, /device:TPU:0, one launch (start us, length us, event | category | flops | bytes accessed | tf_op | source)
XLA Modules:
  0.0 553.5 jit_solution(2809518770260602250)
XLA Ops:
  6.5 0.0 copy-start
  6.5 0.0 reduce-scatter.2.cloned.1.call-start
  6.5 1.4 copy-done
  7.9 0.0 copy-start.2
  7.9 4.9 convolution_bitcast_fusion
  12.8 0.0 copy-done.2
  12.8 2.8 convolution_bitcast_fusion.1
  15.6 4.2 pad_maximum_fusion
  19.8 14.9 %copy.4 = f32[768,2,1500]{2,1,0:T(2,128)} copy(f32[768,2,1500]{0,2,1:T(8,128)} %pad_maximum_fusion) | data formatting | bytes 18432000 | tf_op jit(solution)/shard_map/stack | solution.py:24
  34.7 12.3 %reshape.3 = f32[1536,1500]{1,0:T(8,128)} reshape(f32[768,2,1500]{2,1,0:T(2,128)} %copy.4) | data formatting | bytes 18432000 | tf_op jit(solution)/shard_map/reshape | solution.py:24
  47.0 371.0 %all-reduce.1 = bf16[1536,1500]{1,0:T(8,128)(2,1)} all-reduce(f32[1536,1500]{1,0:T(8,128)} %reshape.3), channel_id=1, replica_groups=mesh['basis'=8,'aux'=16] {'basis'}, use_global_device_ids=true, to_apply=%region_0.0 | all-reduce | flops 2304000 | bytes 13824000 | tf_op jit(solution)/shard_map/psum | solution.py:25
  418.0 21.4 %fusion.6 = f32[1536,3000]{1,0:T(8,128)} fusion(bf16[1536,1500]{1,0:T(8,128)(2,1)} %all-reduce.1, bf16[1500,3000]{0,1:T(8,128)(2,1)} %param.5), kind=kOutput, calls=%fused_computation.9 | convolution fusion | flops 13824000000 | bytes 32040000 | tf_op jit(solution)/shard_map/dot_general | solution.py:14
  439.4 0.0 reduce-scatter.2.cloned.1.call-update
  439.4 0.0 copy-start.1
  439.4 107.3 %reduce-scatter.2.cloned.1.call-done = f32[96,3000]{1,0:T(8,128)} async-done(((f32[1536,3000]{1,0:T(8,128)}), f32[96,3000]{1,0:T(8,128)}) %reduce-scatter.2.cloned.1.call-update) | async-done | bytes 1152016 | tf_op jit(solution)/shard_map/reduce_scatter | solution.py:26
  546.7 0.0 copy-done.1
Async XLA Ops:
  6.5 1.4 copy-start
  6.5 540.1 %reduce-scatter.2.cloned.1.call-start = ((), (), s32[]{:S(2)}) async-start(), calls=%async_computation.1 | async-start | bytes 20054016 | tf_op jit(solution)/shard_map/reduce_scatter | solution.py:26
  7.9 4.9 copy-start.2
  439.4 107.3 %copy-start.1 = (bf16[1000,768]{1,0:T(8,128)(2,1)S(1)}, bf16[1000,768]{1,0:T(8,128)(2,1)}, u32[]{:S(2)}) copy-start(bf16[1000,768]{1,0:T(8,128)(2,1)} %param.4) | copy-start | bytes 4608004
Sparse Core Ops, SparseCore 0:
  439.5 107.1 reduce-scatter.1
where the time goes:
time: 554 us
  blocking collectives  371 us (67%)
  waiting for transfers between devices  107 us (19%)
  matrix products  29.1 us (5%)
  local copies, waits for them, and re-layouts  28.6 us (5%)
  between operations  13.4 us (2%)
    psum x1, blocking collectives, on_device(): pair_ints = lax.psum(partial_ints, 'basis').astype(jnp.bfloat16)  371 us
    reduce_scatter x1, waiting for transfers between devices, on_device(): lax.psum_scatter(metric_apply(pair_ints, metric_factor), 'aux', scatter_d...  107 us
    dot_general x1, matrix products, metric_apply(): return jnp.dot(rows_all, metric_factor, preferred_element_type=jnp.float32)  21.4 us
    another operation x1, local copies, waits for them, and re-layouts, on_device(): partial_ints = jnp.stack(blocks, axis=1).reshape(n_vir * n_occ, width)  14.9 us
    reshape x1, local copies, waits for them, and re-layouts, on_device(): partial_ints = jnp.stack(blocks, axis=1).reshape(n_vir * n_occ, width)  12.3 us
  transfers between devices with their start and end apart: 1, of which 1 were waited for; matrix products, arithmetic and copies ran while one was open for 0% of the time, Pallas kernels for 0%

commit v1 on v0

v1 whole, which is shorter than its diff:
```python
import jax
import jax.numpy as jnp
from jax import lax
from jax.experimental import pallas as pl
from jax.experimental.pallas import tpu as pltpu
from jax.sharding import PartitionSpec as P

NY, NH, NL, NZ, NC = 4, 2, 2, 4, 2
PARTS = (4, 4, 4)
SCALE = 16.0
TILE = 512

SWAP_H = [(i, i ^ 1) for i in range(NY * NH)]
SWAP_CORE = [(i, i ^ 1) for i in range(NL * NZ * NC)]
SWAP_L = [(i, i ^ (NZ * NC)) for i in range(NL * NZ * NC)]


def on_y(x, step):
    pairs = [(y * NH + h, (y + step) % NY * NH + h) for y in range(NY) for h in range(NH)]
    return lax.ppermute(x, "basis", pairs)


def on_z(x, step):
    pairs = [
        ((l * NZ + z) * NC + k, (l * NZ + (z + step) % NZ) * NC + k)
        for l in range(NL)
        for z in range(NZ)
        for k in range(NC)
    ]
    return lax.ppermute(x, "aux", pairs)


def places():
    basis, aux = lax.axis_index("basis"), lax.axis_index("aux")
    return basis // NH, aux // (NZ * NC), aux // NC % NZ, aux % NC


def after(x, earlier):
    return lax.optimization_barrier((x, earlier))[0]


def f32(x):
    return x.astype(jnp.float32)


def b16(x):
    return x.astype(jnp.bfloat16)


def picked(virt_coeffs, quarter, start, rows):
    y, l, z, k = places()
    n_vir = virt_coeffs.shape[1]
    size = NY * NC * NZ * NL * rows
    at = lax.broadcasted_iota(jnp.int32, (n_vir, size), 1)
    r, at = at % rows, at // rows
    ll, at = at % NL, at // NL
    zz, at = at % NZ, at // NZ
    kk, yy = at % NC, at // NC
    place = ((l ^ (1 - ll)) * NZ + (z + zz + 1) % NZ) * NC + (k ^ kk)
    column = (place * NY + (y + yy + 1) % NY) * quarter + start + r
    pick = b16(lax.broadcasted_iota(jnp.int32, (n_vir, size), 0) == column)
    return b16(jnp.dot(virt_coeffs, pick, preferred_element_type=jnp.float32))


def placed_rows(done, quarter, start, rows, n_occ):
    y = places()[0]
    size = NY * n_occ * rows
    shape = (NY * quarter * n_occ, size)
    at = lax.broadcasted_iota(jnp.int32, shape, 1)
    r, at = at % rows, at // rows
    i, yy = at % n_occ, at // n_occ
    row = (((y + yy + 1) % NY) * quarter + start + r) * n_occ + i
    place = f32(lax.broadcasted_iota(jnp.int32, shape, 0) == row)
    return jnp.dot(place, done, precision=lax.Precision.HIGHEST, preferred_element_type=jnp.float32)


def partial_sums(half_ints, cols):
    n_occ, _, width = half_ints.shape
    per = cols.shape[1] // NY
    blocks = [
        (lax.dot_general(cols, half_ints[i], (((0,), (0,)), ((), ())), preferred_element_type=jnp.float32) * SCALE)
        .astype(jnp.float16)
        .reshape(NY, per, width)
        for i in range(n_occ)
    ]
    return [jnp.stack([blocks[i][n] for i in range(n_occ)]) for n in range(NY)]


def fit_kernel(near_u, far_u, back_u, mine_u, own, other, near, far, back, mine, rows):
    units = (near_u, far_u, back_u, mine_u)
    n_occ, _, r, _ = mine_u.shape

    @pl.when(pl.program_id(0) == 0)
    def _():
        for n, unit in enumerate(units):
            for i in range(n_occ):
                g = n * n_occ + i
                for h in range(2):
                    rows[h, g * r : (g + 1) * r, :] = unit[i, h]

    by_columns = (((1,), (1,)), ((), ()))
    total = lax.dot_general(rows[0], own[...], by_columns, preferred_element_type=jnp.float32)
    total = total + lax.dot_general(rows[1], other[...], by_columns, preferred_element_type=jnp.float32)
    one = r // NZ
    for z, out in enumerate((near, far, back, mine)):
        groups = [total[g * r + z * one : g * r + (z + 1) * one] for g in range(NY * n_occ)]
        out[...] = jnp.concatenate(groups, 0).astype(out.dtype)


def fit(units, own, other):
    n_occ, _, r, width = units[0].shape
    n_cols = own.shape[0]
    n_rows = NY * n_occ * r
    unit = pl.BlockSpec(units[0].shape, lambda q: (0, 0, 0, 0))
    factor = pl.BlockSpec((TILE, width), lambda q: (q, 0))
    out = pl.BlockSpec((n_rows // NZ, TILE), lambda q: (0, q))
    shape = lambda d: jax.ShapeDtypeStruct((n_rows // NZ, n_cols), d)
    return pl.pallas_call(
        fit_kernel,
        grid=(pl.cdiv(n_cols, TILE),),
        in_specs=[unit] * NY + [factor] * 2,
        out_specs=[out] * NZ,
        out_shape=[shape(jnp.bfloat16)] * 3 + [shape(jnp.float32)],
        scratch_shapes=[pltpu.VMEM((2, n_rows, width), jnp.bfloat16)],
        compiler_params=pltpu.CompilerParams(vmem_limit_bytes=40 << 20),
        cost_estimate=pl.CostEstimate(
            flops=4 * n_rows * width * n_cols, bytes_accessed=4 * width * n_cols + 2 * n_rows * n_cols, transcendentals=0
        ),
    )(*units, own, other)


def on_device(half_ints, virt_coeffs, metric_factor):
    n_occ = half_ints.shape[0]
    n_vir = virt_coeffs.shape[1]
    width = metric_factor.shape[1]
    quarter = n_vir // (NL * NZ * NC * NY)
    starts = [sum(PARTS[:p]) for p in range(len(PARTS))]
    parts = range(len(PARTS))

    sums = [partial_sums(half_ints, picked(virt_coeffs, quarter, starts[p], PARTS[p])) for p in parts]
    other_factor = lax.ppermute(metric_factor, "aux", SWAP_CORE)
    own_t, other_t = metric_factor.T, other_factor.T

    gathered, previous = [], None
    for p in parts:
        near, far, back, mine = sums[p]
        if previous is not None:
            near, far, back = after((near, far, back), previous)
        got = [on_y(near, 1), on_y(back, 3), on_y(far, 2)]
        previous = got
        total = f32(mine) + f32(got[0]) + f32(got[1]) + f32(got[2])
        pair = b16((total + f32(lax.ppermute(total.astype(jnp.float16), "basis", SWAP_H))) * (1 / SCALE))
        keep = pair.shape[1] // NC
        swapped = lax.ppermute(pair[:, keep:], "aux", SWAP_CORE)
        block = jnp.stack([pair[:, :keep], swapped], axis=1)
        gathered.append([on_y(block, 3), on_y(block, 2), on_y(block, 1), block])

    results = []
    for p in parts:
        near, far, back, mine = fit(gathered[p], own_t, other_t)
        total = mine + f32(on_z(near, 1)) + f32(on_z(back, 3)) + f32(on_z(far, 2))
        total = total.reshape(NY * n_occ, NL, PARTS[p], width)
        done = total[:, 1] + f32(lax.ppermute(b16(total[:, 0]), "aux", SWAP_L))
        results.append(placed_rows(done.reshape(-1, width), quarter, starts[p], PARTS[p], n_occ))
    return sum(results[1:], results[0])


def solution(mesh):
    placed = (P(None, "basis", "aux"), P("basis", None), P("aux", "basis"))
    return jax.shard_map(
        on_device, mesh=mesh, in_specs=placed, out_specs=P("aux", "basis"), check_vma=False
    )
```

time: 554 us -> 203 us (0.37)
  blocking collectives: 371 us -> 0 us
  starting transfers between devices: 0.01 us -> 59.2 us
  waiting for transfers between devices: 107 us -> 79.8 us
  Pallas kernels: 0 us -> 27.1 us
  matrix products: 29.1 us -> 11.1 us
  local copies, waits for them, and re-layouts: 28.6 us -> 14.4 us
  between operations: 13.4 us -> 0.59 us
  other arithmetic: 4.19 us -> 9.76 us
    psum x1 -> x0, blocking collectives: 371 us -> none  [on_device(): pair_ints = lax.psum(partial_ints, 'basis').astype(jnp.bfloat16)]
    reduce_scatter x1 -> x0, waiting for transfers between devices: 107 us -> none  [on_device(): lax.psum_scatter(metric_apply(pair_ints, metric_factor), 'aux', scatter_d...]
    ppermute x0 -> x37, waiting for transfers between devices: none -> 79.8 us  [the longest x18 51.2 us: on_y(): return lax.ppermute(x, 'basis', pairs)]
    ppermute x0 -> x37, starting transfers between devices: none -> 59.2 us  [the longest x18 33.7 us: on_y(): return lax.ppermute(x, 'basis', pairs)]
    pallas_call x0 -> x3, Pallas kernels: none -> 27.1 us  [fit(): pl.pallas_call(fit_kernel, grid=(pl.cdiv(n_cols, TILE),), in_specs=[unit]...]
    dot_general x3 -> x12, matrix products: 29.1 us -> 11.1 us  [the longest x6 6.03 us: partial_sums(): lax.dot_general(cols, half_ints[i], (((0,), (0,)), ((), ())), preferred_e...]
    another operation x1 -> x5, local copies, waits for them, and re-layouts: 14.9 us -> 0.14 us  [on_device(): block = jnp.stack([pair[:, :keep], swapped], axis=1)]
    reshape x1 -> x6, local copies, waits for them, and re-layouts: 12.3 us -> 4.03 us  [the longest x3 3.62 us: on_device(): total = total.reshape(NY * n_occ, NL, PARTS[p], width)]
  transfers between devices with their start and end apart: 1 -> 37, of which waited for: 1 -> 18; matrix products, arithmetic and copies ran while one was open for 0% -> 10% of each run, Pallas kernels for 0% -> 13%
where the time goes in v1:
time: 203 us; the launch traced here: 202 us
  waiting for transfers between devices  79.8 us (39%)
  starting transfers between devices  59.2 us (29%)
  Pallas kernels  27.1 us (13%)
  local copies, waits for them, and re-layouts  14.4 us (7%)
  matrix products  11.1 us (5%)
  other arithmetic  9.76 us (5%)
    ppermute x18, waiting for transfers between devices, on_y(): return lax.ppermute(x, 'basis', pairs)  51.2 us
    ppermute x18, starting transfers between devices, on_y(): return lax.ppermute(x, 'basis', pairs)  33.7 us
    pallas_call x3, Pallas kernels, fit(): pl.pallas_call(fit_kernel, grid=(pl.cdiv(n_cols, TILE),), in_specs=[unit]...  27.1 us
    ppermute x9, starting transfers between devices, on_z(): return lax.ppermute(x, 'aux', pairs)  14.6 us
    ppermute x9, waiting for transfers between devices, on_z(): return lax.ppermute(x, 'aux', pairs)  14.3 us
    ppermute x3, waiting for transfers between devices, on_device(): lax.ppermute(total.astype(jnp.float16), 'basis', SWAP_H)  11.2 us
    unnamed x30, local copies, waits for them, and re-layouts  7.08 us
    ppermute x3, starting transfers between devices, on_device(): lax.ppermute(total.astype(jnp.float16), 'basis', SWAP_H)  6.98 us
  transfers between devices with their start and end apart: 37, of which 18 were waited for; matrix products, arithmetic and copies ran while one was open for 10% of the time, Pallas kernels for 13%

profile of v1, /device:TPU:0, one launch (start us, length us, event | category | flops | bytes accessed | tf_op | source)
XLA Modules:
  0.0 202.0 jit_solution(14200499651424501979)
XLA Ops:
  0.1 1.3 copy-done
  2.1 2.1 %copy-done.8 = bf16[2,1000,1500]{2,1,0:T(8,128)(2,1)S(1)} copy-done((bf16[2,1000,1500]{2,1,0:T(8,128)(2,1)S(1)}, bf16[2,1000,1500]{2,1,0:T(8,128)(2,1)}, u32[]{:S(2)}) %copy-start.8) | copy-done | bytes 6000024
  6.6 1.7 collective-permute-start
  8.4 1.6 collective-permute-start.1
  10.1 2.1 %collective-permute-start.2 = (f16[2,64,1500]{2,1,0:T(8,128)(2,1)S(1)}, f16[2,64,1500]{2,1,0:T(8,128)(2,1)S(1)}, u32[]{:S(2)}, u32[]{:S(2)}) collective-permute-start(f16[2,64,1500]{2,1,0:T(8,128)(2,1)S(1)} %pad_maximum_fusion.2), channel_id=1, source_target_pairs={{0,64},{16,80},{32,96},{48,112},{64,0},{80,16},{96,32},{112,48},{1... | collective-permute-start | bytes 1152008 | tf_op jit(solution)/shard_map/ppermute | solution.py:20
  19.0 1.5 collective-permute-done.1
  20.5 7.9 %collective-permute-done.2 = f16[2,64,1500]{2,1,0:T(8,128)(2,1)S(1)} collective-permute-done((f16[2,64,1500]{2,1,0:T(8,128)(2,1)S(1)}, f16[2,64,1500]{2,1,0:T(8,128)(2,1)S(1)}, u32[]{:S(2)}, u32[]{:S(2)}) %collective-permute-start.2) | collective-permute-done | bytes 384032 | tf_op jit(solution)/shard_map/ppermute | solution.py:20
  28.5 1.3 collective-permute-start.13
  29.8 1.9 collective-permute-start.14
  32.1 3.1 %collective-permute-start.3 = (f16[2,64,1500]{2,1,0:T(8,128)(2,1)S(1)}, f16[2,64,1500]{2,1,0:T(8,128)(2,1)S(1)}, u32[]{:S(2)}, u32[]{:S(2)}) collective-permute-start(f16[2,64,1500]{2,1,0:T(8,128)(2,1)S(1)} %fusion.105), channel_id=1, source_target_pairs={{0,16},{16,0},{32,48},{48,32},{64,80},{80,64},{96,112},{112,96},{1... | collective-permute-start | bytes 1152008 | tf_op jit(solution)/shard_map/ppermute | solution.py:152
  35.2 12.8 %collective-permute-done.13 = f16[2,64,1500]{2,1,0:T(8,128)(2,1)S(1)} collective-permute-done((f16[2,64,1500]{2,1,0:T(8,128)(2,1)S(1)}, f16[2,64,1500]{2,1,0:T(8,128)(2,1)S(1)}, u32[]{:S(2)}, u32[]{:S(2)}) %collective-permute-start.13) | collective-permute-done | bytes 384032 | tf_op jit(solution)/shard_map/ppermute | solution.py:20
  48.3 3.3 %collective-permute-start.16 = (f16[2,64,1500]{2,1,0:T(8,128)(2,1)S(1)}, f16[2,64,1500]{2,1,0:T(8,128)(2,1)S(1)}, u32[]{:S(2)}, u32[]{:S(2)}) collective-permute-start(f16[2,64,1500]{2,1,0:T(8,128)(2,1)S(1)} %fusion.106), channel_id=1, source_target_pairs={{0,16},{16,0},{32,48},{48,32},{64,80},{80,64},{96,112},{112,96},{1... | collective-permute-start | bytes 1152008 | tf_op jit(solution)/shard_map/ppermute | solution.py:152
  53.0 2.4 %collective-permute-start.26 = (f16[2,64,1500]{2,1,0:T(8,128)(2,1)S(1)}, f16[2,64,1500]{2,1,0:T(8,128)(2,1)S(1)}, u32[]{:S(2)}, u32[]{:S(2)}) collective-permute-start(f16[2,64,1500]{2,1,0:T(8,128)(2,1)S(1)} %pad_maximum_fusion.10), channel_id=1, source_target_pairs={{0,96},{16,112},{32,0},{48,16},{64,32},{80,48},{96,64},{112,80},{1... | collective-permute-start | bytes 1152008 | tf_op jit(solution)/shard_map/ppermute | solution.py:20
  55.4 2.9 %collective-permute-done.16 = f16[2,64,1500]{2,1,0:T(8,128)(2,1)S(1)} collective-permute-done((f16[2,64,1500]{2,1,0:T(8,128)(2,1)S(1)}, f16[2,64,1500]{2,1,0:T(8,128)(2,1)S(1)}, u32[]{:S(2)}, u32[]{:S(2)}) %collective-permute-start.16) | collective-permute-done | bytes 384032 | tf_op jit(solution)/shard_map/ppermute | solution.py:152
  58.3 1.8 collective-permute-start.27
  60.4 4.4 %collective-permute-done.25 = f16[2,64,1500]{2,1,0:T(8,128)(2,1)S(1)} collective-permute-done((f16[2,64,1500]{2,1,0:T(8,128)(2,1)S(1)}, f16[2,64,1500]{2,1,0:T(8,128)(2,1)S(1)}, u32[]{:S(2)}, u32[]{:S(2)}) %collective-permute-start.25) | collective-permute-done | bytes 384032 | tf_op jit(solution)/shard_map/ppermute | solution.py:20
  64.8 7.7 %collective-permute-done.26 = f16[2,64,1500]{2,1,0:T(8,128)(2,1)S(1)} collective-permute-done((f16[2,64,1500]{2,1,0:T(8,128)(2,1)S(1)}, f16[2,64,1500]{2,1,0:T(8,128)(2,1)S(1)}, u32[]{:S(2)}, u32[]{:S(2)}) %collective-permute-start.26) | collective-permute-done | bytes 384032 | tf_op jit(solution)/shard_map/ppermute | solution.py:20
  72.6 1.9 collective-permute-done.27
  75.4 1.9 collective-permute-start.5
  77.2 1.4 collective-permute-start.6
  78.7 8.3 %collective-permute-done.28 = f16[2,64,1500]{2,1,0:T(8,128)(2,1)S(1)} collective-permute-done((f16[2,64,1500]{2,1,0:T(8,128)(2,1)S(1)}, f16[2,64,1500]{2,1,0:T(8,128)(2,1)S(1)}, u32[]{:S(2)}, u32[]{:S(2)}) %collective-permute-start.28) | collective-permute-done | bytes 384032 | tf_op jit(solution)/shard_map/ppermute | solution.py:152
  87.0 1.5 collective-permute-start.18
  88.9 1.5 collective-permute-start.19
  90.8 5.8 %collective-permute-start.20 = (bf16[2,2,32,1500]{3,2,0,1:T(8,128)(2,1)S(1)}, bf16[2,2,32,1500]{3,2,0,1:T(8,128)(2,1)S(1)}, u32[]{:S(2)}, u32[]{:S(2)}) collective-permute-start(bf16[2,2,32,1500]{3,2,0,1:T(8,128)(2,1)S(1)} %pad_maximum_fusion.7), channel_id=1, source_target_pairs={{0,32},{16,48},{32,64},{48,80},{64,96},{80,112},{96,0},{112,16},{1... | collective-permute-start | bytes 1152008 | tf_op jit(solution)/shard_map/ppermute | solution.py:20
  96.6 2.7 %collective-permute-done.7 = bf16[2,2,32,1500]{3,2,0,1:T(8,128)(2,1)S(1)} collective-permute-done((bf16[2,2,32,1500]{3,2,0,1:T(8,128)(2,1)S(1)}, bf16[2,2,32,1500]{3,2,0,1:T(8,128)(2,1)S(1)}, u32[]{:S(2)}, u32[]{:S(2)}) %collective-permute-start.7) | collective-permute-done | bytes 384032 | tf_op jit(solution)/shard_map/ppermute | solution.py:20
  99.5 1.3 collective-permute-done.29
  101.4 3.0 %collective-permute-done.18 = bf16[2,2,32,1500]{3,2,0,1:T(8,128)(2,1)S(1)} collective-permute-done((bf16[2,2,32,1500]{3,2,0,1:T(8,128)(2,1)S(1)}, bf16[2,2,32,1500]{3,2,0,1:T(8,128)(2,1)S(1)}, u32[]{:S(2)}, u32[]{:S(2)}) %collective-permute-start.18) | collective-permute-done | bytes 384032 | tf_op jit(solution)/shard_map/ppermute | solution.py:20
  105.6 2.1 %collective-permute-done.19 = bf16[2,2,32,1500]{3,2,0,1:T(8,128)(2,1)S(1)} collective-permute-done((bf16[2,2,32,1500]{3,2,0,1:T(8,128)(2,1)S(1)}, bf16[2,2,32,1500]{3,2,0,1:T(8,128)(2,1)S(1)}, u32[]{:S(2)}, u32[]{:S(2)}) %collective-permute-start.19) | collective-permute-done | bytes 384032 | tf_op jit(solution)/shard_map/ppermute | solution.py:20
  107.7 5.8 %collective-permute-start.32 = (bf16[2,2,32,1500]{3,2,1,0:T(8,128)(2,1)S(1)}, bf16[2,2,32,1500]{3,2,1,0:T(8,128)(2,1)S(1)}, u32[]{:S(2)}, u32[]{:S(2)}) collective-permute-start(bf16[2,2,32,1500]{3,2,1,0:T(8,128)(2,1)S(1)} %pad_maximum_fusion.11.mine_u), channel_id=1, source_target_pairs={{0,32},{16,48},{32,64},{48,80},{64,96},{80,112},{96,0},{112,16},{1... | collective-permute-start | bytes 1152008 | tf_op jit(solution)/shard_map/ppermute | solution.py:20
  113.5 6.7 %collective-permute-done.20 = bf16[2,2,32,1500]{3,2,0,1:T(8,128)(2,1)S(1)} collective-permute-done((bf16[2,2,32,1500]{3,2,0,1:T(8,128)(2,1)S(1)}, bf16[2,2,32,1500]{3,2,0,1:T(8,128)(2,1)S(1)}, u32[]{:S(2)}, u32[]{:S(2)}) %collective-permute-start.20) | collective-permute-done | bytes 384032 | tf_op jit(solution)/shard_map/ppermute | solution.py:20
  120.3 3.6 %copy-done.2 = bf16[1500,3000]{0,1:T(8,128)(2,1)} copy-done((bf16[1500,3000]{0,1:T(8,128)(2,1)}, bf16[1500,3000]{0,1:T(8,128)(2,1)S(1)}, u32[]{:S(2)}) %copy-start.2) | copy-done | bytes 9000024
  123.9 8.6 %shard_map.37 = (bf16[64,3000]{1,0:T(8,128)(2,1)S(1)}, bf16[64,3000]{1,0:T(8,128)(2,1)S(1)}, bf16[64,3000]{1,0:T(8,128)(2,1)S(1)}, f32[64,3000]{1,0:T(8,128)S(1)}) custom-call(bf16[2,2,32,1500]{3,2,1,0:T(8,128)(2,1)S(1)} %copy.6.near_u, bf16[2,2,32,1500]{3,2,1,0:T(8,128)(2,1)S(1)} %copy.7.far_u, bf16[2,2,32,1500]{3,2,1,0:T(8,128)(2,1)S(1)} %copy.8.back_u, ...), custom_call_target="tpu_custom_call" | custom-call | flops 4608000000 | bytes 19536000 | tf_op jit(solution)/shard_map/pallas_call | solution.py:118
  132.5 4.1 %collective-permute-start.10 = (bf16[64,3000]{1,0:T(8,128)(2,1)S(1)}, bf16[64,3000]{1,0:T(8,128)(2,1)S(1)}, u32[]{:S(2)}, u32[]{:S(2)}) collective-permute-start(bf16[64,3000]{1,0:T(8,128)(2,1)S(1)} %get-tuple-element.25), channel_id=1, source_target_pairs={{0,6},{1,7},{2,0},{3,1},{4,2},{5,3},{6,4},{7,5},{8,14},{9,15},{10,... | collective-permute-start | bytes 1152008 | tf_op jit(solution)/shard_map/ppermute | solution.py:30
  136.7 9.2 %shard_map.38 = (bf16[64,3000]{1,0:T(8,128)(2,1)}, bf16[64,3000]{1,0:T(8,128)(2,1)S(1)}, bf16[64,3000]{1,0:T(8,128)(2,1)S(1)}, f32[64,3000]{1,0:T(8,128)S(1)}) custom-call(bf16[2,2,32,1500]{3,2,1,0:T(8,128)(2,1)S(1)} %copy.13.near_u, bf16[2,2,32,1500]{3,2,1,0:T(8,128)(2,1)S(1)} %copy.14.far_u, bf16[2,2,32,1500]{3,2,1,0:T(8,128)(2,1)S(1)} %copy.15.back_u, ...), custom_call_target="tpu_custom_call" | custom-call | flops 4608000000 | bytes 19536000 | tf_op jit(solution)/shard_map/pallas_call | solution.py:118
  147.1 2.2 %collective-permute-start.21 = (bf16[64,3000]{1,0:T(8,128)(2,1)}, bf16[64,3000]{1,0:T(8,128)(2,1)S(1)}, u32[]{:S(2)}, u32[]{:S(2)}) collective-permute-start(bf16[64,3000]{1,0:T(8,128)(2,1)} %get-tuple-element.31), channel_id=1, source_target_pairs={{0,2},{1,3},{2,4},{3,5},{4,6},{5,7},{6,0},{7,1},{8,10},{9,11},{10,... | collective-permute-start | bytes 1152008 | tf_op jit(solution)/shard_map/ppermute | solution.py:30
  150.4 9.3 %shard_map.39 = (bf16[64,3000]{1,0:T(8,128)(2,1)}, bf16[64,3000]{1,0:T(8,128)(2,1)S(1)}, bf16[64,3000]{1,0:T(8,128)(2,1)}, f32[64,3000]{1,0:T(8,128)S(1)}) custom-call(bf16[2,2,32,1500]{3,2,1,0:T(8,128)(2,1)S(1)} %collective-permute-done.30.near_u, bf16[2,2,32,1500]{3,2,1,0:T(8,128)(2,1)S(1)} %collective-permute-done.31.far_u, ...), custom_call_target="tpu_custom_call" | custom-call | flops 4608000000 | bytes 19536000 | tf_op jit(solution)/shard_map/pallas_call | solution.py:118
  161.3 2.7 %collective-permute-start.34 = (bf16[64,3000]{1,0:T(8,128)(2,1)}, bf16[64,3000]{1,0:T(8,128)(2,1)}, u32[]{:S(2)}, u32[]{:S(2)}) collective-permute-start(bf16[64,3000]{1,0:T(8,128)(2,1)} %get-tuple-element.39), channel_id=1, source_target_pairs={{0,6},{1,7},{2,0},{3,1},{4,2},{5,3},{6,4},{7,5},{8,14},{9,15},{10,... | collective-permute-start | bytes 1152008 | tf_op jit(solution)/shard_map/ppermute | solution.py:30
  165.1 2.3 %reshape.51 = f32[8,2,4,3000]{3,2,1,0:T(4,128)} reshape(f32[64,3000]{1,0:T(8,128)} %convert_add_fusion.4) | data formatting | bytes 1536000 | tf_op jit(solution)/shard_map/reshape | solution.py:162
  168.4 6.3 %collective-permute-done.21 = bf16[64,3000]{1,0:T(8,128)(2,1)S(1)} collective-permute-done((bf16[64,3000]{1,0:T(8,128)(2,1)}, bf16[64,3000]{1,0:T(8,128)(2,1)S(1)}, u32[]{:S(2)}, u32[]{:S(2)}) %collective-permute-start.21) | collective-permute-done | bytes 384032 | tf_op jit(solution)/shard_map/ppermute | solution.py:30
  174.7 1.6 collective-permute-start.35
  176.4 1.5 collective-permute-start.12
  177.9 1.4 convert_add_fusion.2
  180.2 3.8 %collective-permute-done.33 = bf16[64,3000]{1,0:T(8,128)(2,1)} collective-permute-done((bf16[64,3000]{1,0:T(8,128)(2,1)}, bf16[64,3000]{1,0:T(8,128)(2,1)}, u32[]{:S(2)}, u32[]{:S(2)}) %collective-permute-start.33) | collective-permute-done | bytes 384032 | tf_op jit(solution)/shard_map/ppermute | solution.py:30
  184.0 4.3 %collective-permute-done.35 = bf16[64,3000]{1,0:T(8,128)(2,1)} collective-permute-done((bf16[64,3000]{1,0:T(8,128)(2,1)S(1)}, bf16[64,3000]{1,0:T(8,128)(2,1)}, u32[]{:S(2)}, u32[]{:S(2)}) %collective-permute-start.35) | collective-permute-done | bytes 384032 | tf_op jit(solution)/shard_map/ppermute | solution.py:30
  188.2 1.4 convert_add_fusion
  191.8 1.6 collective-permute-start.36
  195.8 1.9 collective-permute-done.36
  200.2 1.8 fusion
  (129 shorter events, 30.0 us)
Async XLA Ops:
  4.1 8.2 %slice-start = ((s8[9216000]{0:T(1024)(128)(4,1)}), s8[4194304]{0:T(1024)(128)(4,1)S(1)}, s32[]{:S(2)}) async-start(s8[9216000]{0:T(1024)(128)(4,1)} %bitcast.135), calls=%async_computation | async-start | bytes 8388608
  4.1 8.2 %slice-start.1 = ((s8[9216000]{0:T(1024)(128)(4,1)}), s8[4194304]{0:T(1024)(128)(4,1)S(1)}, s32[]{:S(2)}) async-start(s8[9216000]{0:T(1024)(128)(4,1)} %bitcast.135), calls=%async_computation.1 | async-start | bytes 8388608
  5.2 7.1 %slice-start.2 = ((s8[9216000]{0:T(1024)(128)(4,1)}), s8[827392]{0:T(1024)(128)(4,1)S(1)}, s32[]{:S(2)}) async-start(s8[9216000]{0:T(1024)(128)(4,1)} %bitcast.135), calls=%async_computation.2 | async-start | bytes 1654784
  6.6 12.4 %collective-permute-start = (f16[2,64,1500]{2,1,0:T(8,128)(2,1)S(1)}, f16[2,64,1500]{2,1,0:T(8,128)(2,1)S(1)}, u32[]{:S(2)}, u32[]{:S(2)}) collective-permute-start(f16[2,64,1500]{2,1,0:T(8,128)(2,1)S(1)} %pad_maximum_fusion), channel_id=1, source_target_pairs={{0,32},{16,48},{32,64},{48,80},{64,96},{80,112},{96,0},{112,16},{1... | collective-permute-start | bytes 1152008 | tf_op jit(solution)/shard_map/ppermute | solution.py:20
  8.4 12.1 %collective-permute-start.1 = (f16[2,64,1500]{2,1,0:T(8,128)(2,1)S(1)}, f16[2,64,1500]{2,1,0:T(8,128)(2,1)S(1)}, u32[]{:S(2)}, u32[]{:S(2)}) collective-permute-start(f16[2,64,1500]{2,1,0:T(8,128)(2,1)S(1)} %pad_maximum_fusion.1), channel_id=1, source_target_pairs={{0,96},{16,112},{32,0},{48,16},{64,32},{80,48},{96,64},{112,80},{1... | collective-permute-start | bytes 1152008 | tf_op jit(solution)/shard_map/ppermute | solution.py:20
  10.1 18.3 %collective-permute-start.2 = (f16[2,64,1500]{2,1,0:T(8,128)(2,1)S(1)}, f16[2,64,1500]{2,1,0:T(8,128)(2,1)S(1)}, u32[]{:S(2)}, u32[]{:S(2)}) collective-permute-start(f16[2,64,1500]{2,1,0:T(8,128)(2,1)S(1)} %pad_maximum_fusion.2), channel_id=1, source_target_pairs={{0,64},{16,80},{32,96},{48,112},{64,0},{80,16},{96,32},{112,48},{1... | collective-permute-start | bytes 1152008 | tf_op jit(solution)/shard_map/ppermute | solution.py:20
  12.3 108.0 %collective-permute-start.8 = (bf16[1500,3000]{0,1:T(8,128)(2,1)S(1)}, bf16[1500,3000]{0,1:T(8,128)(2,1)S(1)}, u32[]{:S(2)}, u32[]{:S(2)}) collective-permute-start(bf16[1500,3000]{0,1:T(8,128)(2,1)S(1)} %bitcast.136), channel_id=1, source_target_pairs={{0,1},{1,0},{2,3},{3,2},{4,5},{5,4},{6,7},{7,6},{8,9},{9,8},{10,11... | collective-permute-start | bytes 27000008 | tf_op jit(solution)/shard_map/ppermute | solution.py:141
  28.5 19.6 %collective-permute-start.13 = (f16[2,64,1500]{2,1,0:T(8,128)(2,1)S(1)}, f16[2,64,1500]{2,1,0:T(8,128)(2,1)S(1)}, u32[]{:S(2)}, u32[]{:S(2)}) collective-permute-start(f16[2,64,1500]{2,1,0:T(8,128)(2,1)S(1)} %pad_maximum_fusion.4), channel_id=1, source_target_pairs={{0,32},{16,48},{32,64},{48,80},{64,96},{80,112},{96,0},{112,16},{1... | collective-permute-start | bytes 1152008 | tf_op jit(solution)/shard_map/ppermute | solution.py:20
  29.8 18.3 %collective-permute-start.14 = (f16[2,64,1500]{2,1,0:T(8,128)(2,1)S(1)}, f16[2,64,1500]{2,1,0:T(8,128)(2,1)S(1)}, u32[]{:S(2)}, u32[]{:S(2)}) collective-permute-start(f16[2,64,1500]{2,1,0:T(8,128)(2,1)S(1)} %pad_maximum_fusion.6), channel_id=1, source_target_pairs={{0,96},{16,112},{32,0},{48,16},{64,32},{80,48},{96,64},{112,80},{1... | collective-permute-start | bytes 1152008 | tf_op jit(solution)/shard_map/ppermute | solution.py:20
  31.7 16.4 %collective-permute-start.15 = (f16[2,64,1500]{2,1,0:T(8,128)(2,1)S(1)}, f16[2,64,1500]{2,1,0:T(8,128)(2,1)S(1)}, u32[]{:S(2)}, u32[]{:S(2)}) collective-permute-start(f16[2,64,1500]{2,1,0:T(8,128)(2,1)S(1)} %pad_maximum_fusion.5), channel_id=1, source_target_pairs={{0,64},{16,80},{32,96},{48,112},{64,0},{80,16},{96,32},{112,48},{1... | collective-permute-start | bytes 1152008 | tf_op jit(solution)/shard_map/ppermute | solution.py:20
  32.1 19.5 %collective-permute-start.3 = (f16[2,64,1500]{2,1,0:T(8,128)(2,1)S(1)}, f16[2,64,1500]{2,1,0:T(8,128)(2,1)S(1)}, u32[]{:S(2)}, u32[]{:S(2)}) collective-permute-start(f16[2,64,1500]{2,1,0:T(8,128)(2,1)S(1)} %fusion.105), channel_id=1, source_target_pairs={{0,16},{16,0},{32,48},{48,32},{64,80},{80,64},{96,112},{112,96},{1... | collective-permute-start | bytes 1152008 | tf_op jit(solution)/shard_map/ppermute | solution.py:152
  48.1 75.8 %slice-start.3 = ((s8[9216000]{0:T(1024)(128)(4,1)}), s8[4194304]{0:T(1024)(128)(4,1)S(1)}, s32[]{:S(2)}) async-start(s8[9216000]{0:T(1024)(128)(4,1)} %bitcast.137), calls=%async_computation.3 | async-start | bytes 8388608
  48.3 9.9 %collective-permute-start.16 = (f16[2,64,1500]{2,1,0:T(8,128)(2,1)S(1)}, f16[2,64,1500]{2,1,0:T(8,128)(2,1)S(1)}, u32[]{:S(2)}, u32[]{:S(2)}) collective-permute-start(f16[2,64,1500]{2,1,0:T(8,128)(2,1)S(1)} %fusion.106), channel_id=1, source_target_pairs={{0,16},{16,0},{32,48},{48,32},{64,80},{80,64},{96,112},{112,96},{1... | collective-permute-start | bytes 1152008 | tf_op jit(solution)/shard_map/ppermute | solution.py:152
  52.0 71.9 %slice-start.4 = ((s8[9216000]{0:T(1024)(128)(4,1)}), s8[4194304]{0:T(1024)(128)(4,1)S(1)}, s32[]{:S(2)}) async-start(s8[9216000]{0:T(1024)(128)(4,1)} %bitcast.137), calls=%async_computation.4 | async-start | bytes 8388608
  52.0 23.3 %collective-permute-start.4 = (bf16[2,32,1500]{2,1,0:T(8,128)(2,1)S(1)}, bf16[2,32,1500]{2,1,0:T(8,128)(2,1)S(1)}, u32[]{:S(2)}, u32[]{:S(2)}) collective-permute-start(bf16[2,32,1500]{2,1,0:T(8,128)(2,1)S(1)} %get-tuple-element.66), channel_id=1, source_target_pairs={{0,1},{1,0},{2,3},{3,2},{4,5},{5,4},{6,7},{7,6},{8,9},{9,8},{10,11... | collective-permute-start | bytes 576008 | tf_op jit(solution)/shard_map/ppermute | solution.py:154
  52.1 12.7 %collective-permute-start.25 = (f16[2,64,1500]{2,1,0:T(8,128)(2,1)S(1)}, f16[2,64,1500]{2,1,0:T(8,128)(2,1)S(1)}, u32[]{:S(2)}, u32[]{:S(2)}) collective-permute-start(f16[2,64,1500]{2,1,0:T(8,128)(2,1)S(1)} %pad_maximum_fusion.8), channel_id=1, source_target_pairs={{0,32},{16,48},{32,64},{48,80},{64,96},{80,112},{96,0},{112,16},{1... | collective-permute-start | bytes 1152008 | tf_op jit(solution)/shard_map/ppermute | solution.py:20
  53.0 19.6 %collective-permute-start.26 = (f16[2,64,1500]{2,1,0:T(8,128)(2,1)S(1)}, f16[2,64,1500]{2,1,0:T(8,128)(2,1)S(1)}, u32[]{:S(2)}, u32[]{:S(2)}) collective-permute-start(f16[2,64,1500]{2,1,0:T(8,128)(2,1)S(1)} %pad_maximum_fusion.10), channel_id=1, source_target_pairs={{0,96},{16,112},{32,0},{48,16},{64,32},{80,48},{96,64},{112,80},{1... | collective-permute-start | bytes 1152008 | tf_op jit(solution)/shard_map/ppermute | solution.py:20
  58.3 16.2 %collective-permute-start.27 = (f16[2,64,1500]{2,1,0:T(8,128)(2,1)S(1)}, f16[2,64,1500]{2,1,0:T(8,128)(2,1)S(1)}, u32[]{:S(2)}, u32[]{:S(2)}) collective-permute-start(f16[2,64,1500]{2,1,0:T(8,128)(2,1)S(1)} %pad_maximum_fusion.9), channel_id=1, source_target_pairs={{0,64},{16,80},{32,96},{48,112},{64,0},{80,16},{96,32},{112,48},{1... | collective-permute-start | bytes 1152008 | tf_op jit(solution)/shard_map/ppermute | solution.py:20
  64.8 13.8 %collective-permute-start.17 = (bf16[2,32,1500]{2,1,0:T(8,128)(2,1)S(1)}, bf16[2,32,1500]{2,1,0:T(8,128)(2,1)S(1)}, u32[]{:S(2)}, u32[]{:S(2)}) collective-permute-start(bf16[2,32,1500]{2,1,0:T(8,128)(2,1)S(1)} %get-tuple-element.68), channel_id=1, source_target_pairs={{0,1},{1,0},{2,3},{3,2},{4,5},{5,4},{6,7},{7,6},{8,9},{9,8},{10,11... | collective-permute-start | bytes 576008 | tf_op jit(solution)/shard_map/ppermute | solution.py:154
  74.8 12.3 %collective-permute-start.28 = (f16[2,64,1500]{2,1,0:T(8,128)(2,1)S(1)}, f16[2,64,1500]{2,1,0:T(8,128)(2,1)S(1)}, u32[]{:S(2)}, u32[]{:S(2)}) collective-permute-start(f16[2,64,1500]{2,1,0:T(8,128)(2,1)S(1)} %fusion.107), channel_id=1, source_target_pairs={{0,16},{16,0},{32,48},{48,32},{64,80},{80,64},{96,112},{112,96},{1... | collective-permute-start | bytes 1152008 | tf_op jit(solution)/shard_map/ppermute | solution.py:152
  75.4 13.5 %collective-permute-start.5 = (bf16[2,2,32,1500]{3,2,0,1:T(8,128)(2,1)S(1)}, bf16[2,2,32,1500]{3,2,0,1:T(8,128)(2,1)S(1)}, u32[]{:S(2)}, u32[]{:S(2)}) collective-permute-start(bf16[2,2,32,1500]{3,2,0,1:T(8,128)(2,1)S(1)} %pad_maximum_fusion.3), channel_id=1, source_target_pairs={{0,96},{16,112},{32,0},{48,16},{64,32},{80,48},{96,64},{112,80},{1... | collective-permute-start | bytes 1152008 | tf_op jit(solution)/shard_map/ppermute | solution.py:20
  77.2 13.6 %collective-permute-start.6 = (bf16[2,2,32,1500]{3,2,0,1:T(8,128)(2,1)S(1)}, bf16[2,2,32,1500]{3,2,0,1:T(8,128)(2,1)S(1)}, u32[]{:S(2)}, u32[]{:S(2)}) collective-permute-start(bf16[2,2,32,1500]{3,2,0,1:T(8,128)(2,1)S(1)} %pad_maximum_fusion.3), channel_id=1, source_target_pairs={{0,64},{16,80},{32,96},{48,112},{64,0},{80,16},{96,32},{112,48},{1... | collective-permute-start | bytes 1152008 | tf_op jit(solution)/shard_map/ppermute | solution.py:20
  78.6 20.7 %collective-permute-start.7 = (bf16[2,2,32,1500]{3,2,0,1:T(8,128)(2,1)S(1)}, bf16[2,2,32,1500]{3,2,0,1:T(8,128)(2,1)S(1)}, u32[]{:S(2)}, u32[]{:S(2)}) collective-permute-start(bf16[2,2,32,1500]{3,2,0,1:T(8,128)(2,1)S(1)} %pad_maximum_fusion.3), channel_id=1, source_target_pairs={{0,32},{16,48},{32,64},{48,80},{64,96},{80,112},{96,0},{112,16},{1... | collective-permute-start | bytes 1152008 | tf_op jit(solution)/shard_map/ppermute | solution.py:20
  87.0 17.4 %collective-permute-start.18 = (bf16[2,2,32,1500]{3,2,0,1:T(8,128)(2,1)S(1)}, bf16[2,2,32,1500]{3,2,0,1:T(8,128)(2,1)S(1)}, u32[]{:S(2)}, u32[]{:S(2)}) collective-permute-start(bf16[2,2,32,1500]{3,2,0,1:T(8,128)(2,1)S(1)} %pad_maximum_fusion.7), channel_id=1, source_target_pairs={{0,96},{16,112},{32,0},{48,16},{64,32},{80,48},{96,64},{112,80},{1... | collective-permute-start | bytes 1152008 | tf_op jit(solution)/shard_map/ppermute | solution.py:20
  88.8 35.1 %slice-start.5 = ((s8[9216000]{0:T(1024)(128)(4,1)}), s8[827392]{0:T(1024)(128)(4,1)S(1)}, s32[]{:S(2)}) async-start(s8[9216000]{0:T(1024)(128)(4,1)} %bitcast.137), calls=%async_computation.5 | async-start | bytes 1654784
  88.9 18.8 %collective-permute-start.19 = (bf16[2,2,32,1500]{3,2,0,1:T(8,128)(2,1)S(1)}, bf16[2,2,32,1500]{3,2,0,1:T(8,128)(2,1)S(1)}, u32[]{:S(2)}, u32[]{:S(2)}) collective-permute-start(bf16[2,2,32,1500]{3,2,0,1:T(8,128)(2,1)S(1)} %pad_maximum_fusion.7), channel_id=1, source_target_pairs={{0,64},{16,80},{32,96},{48,112},{64,0},{80,16},{96,32},{112,48},{1... | collective-permute-start | bytes 1152008 | tf_op jit(solution)/shard_map/ppermute | solution.py:20
  90.8 29.4 %collective-permute-start.20 = (bf16[2,2,32,1500]{3,2,0,1:T(8,128)(2,1)S(1)}, bf16[2,2,32,1500]{3,2,0,1:T(8,128)(2,1)S(1)}, u32[]{:S(2)}, u32[]{:S(2)}) collective-permute-start(bf16[2,2,32,1500]{3,2,0,1:T(8,128)(2,1)S(1)} %pad_maximum_fusion.7), channel_id=1, source_target_pairs={{0,32},{16,48},{32,64},{48,80},{64,96},{80,112},{96,0},{112,16},{1... | collective-permute-start | bytes 1152008 | tf_op jit(solution)/shard_map/ppermute | solution.py:20
  99.3 1.4 collective-permute-start.29
  100.8 45.1 %collective-permute-start.30 = (bf16[2,2,32,1500]{3,2,1,0:T(8,128)(2,1)S(1)}, bf16[2,2,32,1500]{3,2,1,0:T(8,128)(2,1)S(1)}, u32[]{:S(2)}, u32[]{:S(2)}) collective-permute-start(bf16[2,2,32,1500]{3,2,1,0:T(8,128)(2,1)S(1)} %pad_maximum_fusion.11.mine_u), channel_id=1, source_target_pairs={{0,96},{16,112},{32,0},{48,16},{64,32},{80,48},{96,64},{112,80},{1... | collective-permute-start | bytes 1152008 | tf_op jit(solution)/shard_map/ppermute | solution.py:20
  104.4 42.7 %collective-permute-start.31 = (bf16[2,2,32,1500]{3,2,1,0:T(8,128)(2,1)S(1)}, bf16[2,2,32,1500]{3,2,1,0:T(8,128)(2,1)S(1)}, u32[]{:S(2)}, u32[]{:S(2)}) collective-permute-start(bf16[2,2,32,1500]{3,2,1,0:T(8,128)(2,1)S(1)} %pad_maximum_fusion.11.mine_u), channel_id=1, source_target_pairs={{0,64},{16,80},{32,96},{48,112},{64,0},{80,16},{96,32},{112,48},{1... | collective-permute-start | bytes 1152008 | tf_op jit(solution)/shard_map/ppermute | solution.py:20
  107.7 41.6 %collective-permute-start.32 = (bf16[2,2,32,1500]{3,2,1,0:T(8,128)(2,1)S(1)}, bf16[2,2,32,1500]{3,2,1,0:T(8,128)(2,1)S(1)}, u32[]{:S(2)}, u32[]{:S(2)}) collective-permute-start(bf16[2,2,32,1500]{3,2,1,0:T(8,128)(2,1)S(1)} %pad_maximum_fusion.11.mine_u), channel_id=1, source_target_pairs={{0,32},{16,48},{32,64},{48,80},{64,96},{80,112},{96,0},{112,16},{1... | collective-permute-start | bytes 1152008 | tf_op jit(solution)/shard_map/ppermute | solution.py:20
  120.3 3.6 %copy-start.2 = (bf16[1500,3000]{0,1:T(8,128)(2,1)}, bf16[1500,3000]{0,1:T(8,128)(2,1)S(1)}, u32[]{:S(2)}) copy-start(bf16[1500,3000]{0,1:T(8,128)(2,1)S(1)} %collective-permute-done.8) | copy-start | bytes 27000004
  132.5 27.1 %collective-permute-start.10 = (bf16[64,3000]{1,0:T(8,128)(2,1)S(1)}, bf16[64,3000]{1,0:T(8,128)(2,1)S(1)}, u32[]{:S(2)}, u32[]{:S(2)}) collective-permute-start(bf16[64,3000]{1,0:T(8,128)(2,1)S(1)} %get-tuple-element.25), channel_id=1, source_target_pairs={{0,6},{1,7},{2,0},{3,1},{4,2},{5,3},{6,4},{7,5},{8,14},{9,15},{10,... | collective-permute-start | bytes 1152008 | tf_op jit(solution)/shard_map/ppermute | solution.py:30
  136.6 24.2 %collective-permute-start.11 = (bf16[64,3000]{1,0:T(8,128)(2,1)S(1)}, bf16[64,3000]{1,0:T(8,128)(2,1)S(1)}, u32[]{:S(2)}, u32[]{:S(2)}) collective-permute-start(bf16[64,3000]{1,0:T(8,128)(2,1)S(1)} %get-tuple-element.26), channel_id=1, source_target_pairs={{0,4},{1,5},{2,6},{3,7},{4,0},{5,1},{6,2},{7,3},{8,12},{9,13},{10,... | collective-permute-start | bytes 1152008 | tf_op jit(solution)/shard_map/ppermute | solution.py:30
  145.9 15.4 %collective-permute-start.9 = (bf16[64,3000]{1,0:T(8,128)(2,1)S(1)}, bf16[64,3000]{1,0:T(8,128)(2,1)S(1)}, u32[]{:S(2)}, u32[]{:S(2)}) collective-permute-start(bf16[64,3000]{1,0:T(8,128)(2,1)S(1)} %get-tuple-element.24), channel_id=1, source_target_pairs={{0,2},{1,3},{2,4},{3,5},{4,6},{5,7},{6,0},{7,1},{8,10},{9,11},{10,... | collective-permute-start | bytes 1152008 | tf_op jit(solution)/shard_map/ppermute | solution.py:30
  147.1 27.6 %collective-permute-start.21 = (bf16[64,3000]{1,0:T(8,128)(2,1)}, bf16[64,3000]{1,0:T(8,128)(2,1)S(1)}, u32[]{:S(2)}, u32[]{:S(2)}) collective-permute-start(bf16[64,3000]{1,0:T(8,128)(2,1)} %get-tuple-element.31), channel_id=1, source_target_pairs={{0,2},{1,3},{2,4},{3,5},{4,6},{5,7},{6,0},{7,1},{8,10},{9,11},{10,... | collective-permute-start | bytes 1152008 | tf_op jit(solution)/shard_map/ppermute | solution.py:30
  149.4 27.0 %collective-permute-start.22 = (bf16[64,3000]{1,0:T(8,128)(2,1)S(1)}, bf16[64,3000]{1,0:T(8,128)(2,1)}, u32[]{:S(2)}, u32[]{:S(2)}) collective-permute-start(bf16[64,3000]{1,0:T(8,128)(2,1)S(1)} %get-tuple-element.32), channel_id=1, source_target_pairs={{0,6},{1,7},{2,0},{3,1},{4,2},{5,3},{6,4},{7,5},{8,14},{9,15},{10,... | collective-permute-start | bytes 1152008 | tf_op jit(solution)/shard_map/ppermute | solution.py:30
  159.7 18.2 %collective-permute-start.23 = (bf16[64,3000]{1,0:T(8,128)(2,1)S(1)}, bf16[64,3000]{1,0:T(8,128)(2,1)}, u32[]{:S(2)}, u32[]{:S(2)}) collective-permute-start(bf16[64,3000]{1,0:T(8,128)(2,1)S(1)} %get-tuple-element.33), channel_id=1, source_target_pairs={{0,4},{1,5},{2,6},{3,7},{4,0},{5,1},{6,2},{7,3},{8,12},{9,13},{10,... | collective-permute-start | bytes 1152008 | tf_op jit(solution)/shard_map/ppermute | solution.py:30
  160.8 23.1 %collective-permute-start.33 = (bf16[64,3000]{1,0:T(8,128)(2,1)}, bf16[64,3000]{1,0:T(8,128)(2,1)}, u32[]{:S(2)}, u32[]{:S(2)}) collective-permute-start(bf16[64,3000]{1,0:T(8,128)(2,1)} %get-tuple-element.38), channel_id=1, source_target_pairs={{0,2},{1,3},{2,4},{3,5},{4,6},{5,7},{6,0},{7,1},{8,10},{9,11},{10,... | collective-permute-start | bytes 1152008 | tf_op jit(solution)/shard_map/ppermute | solution.py:30
  161.3 22.7 %collective-permute-start.34 = (bf16[64,3000]{1,0:T(8,128)(2,1)}, bf16[64,3000]{1,0:T(8,128)(2,1)}, u32[]{:S(2)}, u32[]{:S(2)}) collective-permute-start(bf16[64,3000]{1,0:T(8,128)(2,1)} %get-tuple-element.39), channel_id=1, source_target_pairs={{0,6},{1,7},{2,0},{3,1},{4,2},{5,3},{6,4},{7,5},{8,14},{9,15},{10,... | collective-permute-start | bytes 1152008 | tf_op jit(solution)/shard_map/ppermute | solution.py:30
  174.7 13.5 %collective-permute-start.35 = (bf16[64,3000]{1,0:T(8,128)(2,1)S(1)}, bf16[64,3000]{1,0:T(8,128)(2,1)}, u32[]{:S(2)}, u32[]{:S(2)}) collective-permute-start(bf16[64,3000]{1,0:T(8,128)(2,1)S(1)} %get-tuple-element.40), channel_id=1, source_target_pairs={{0,4},{1,5},{2,6},{3,7},{4,0},{5,1},{6,2},{7,3},{8,12},{9,13},{10,... | collective-permute-start | bytes 1152008 | tf_op jit(solution)/shard_map/ppermute | solution.py:30
  176.4 17.1 %collective-permute-start.12 = (bf16[8,4,3000]{2,1,0:T(4,128)(2,1)S(1)}, bf16[8,4,3000]{2,1,0:T(4,128)(2,1)}, u32[]{:S(2)}, u32[]{:S(2)}) collective-permute-start(bf16[8,4,3000]{2,1,0:T(4,128)(2,1)S(1)} %fusion.102), channel_id=1, source_target_pairs={{0,8},{1,9},{2,10},{3,11},{4,12},{5,13},{6,14},{7,15},{8,0},{9,1},... | collective-permute-start | bytes 576008 | tf_op jit(solution)/shard_map/ppermute | solution.py:163
  179.5 8.7 %copy-start.4 = (f32[8,2,4,3000]{3,2,1,0:T(4,128)}, f32[8,2,4,3000]{3,2,1,0:T(4,128)S(1)}, u32[]{:S(2)}) copy-start(f32[8,2,4,3000]{3,2,1,0:T(4,128)S(1)} %reshape.53) | copy-start | bytes 2304004
  179.6 14.9 %collective-permute-start.24 = (bf16[8,4,3000]{2,1,0:T(4,128)(2,1)S(1)}, bf16[8,4,3000]{2,1,0:T(4,128)(2,1)}, u32[]{:S(2)}, u32[]{:S(2)}) collective-permute-start(bf16[8,4,3000]{2,1,0:T(4,128)(2,1)S(1)} %fusion.103), channel_id=1, source_target_pairs={{0,8},{1,9},{2,10},{3,11},{4,12},{5,13},{6,14},{7,15},{8,0},{9,1},... | collective-permute-start | bytes 576008 | tf_op jit(solution)/shard_map/ppermute | solution.py:163
  189.6 3.8 %copy-start.3 = (f32[8,2,4,3000]{3,2,1,0:T(4,128)S(1)}, f32[8,2,4,3000]{3,2,1,0:T(4,128)}, u32[]{:S(2)}) copy-start(f32[8,2,4,3000]{3,2,1,0:T(4,128)} %reshape.51) | copy-start | bytes 2304004
  189.6 4.8 %copy-start.5 = (f32[8,2,4,3000]{3,2,1,0:T(4,128)S(1)}, f32[8,2,4,3000]{3,2,1,0:T(4,128)}, u32[]{:S(2)}) copy-start(f32[8,2,4,3000]{3,2,1,0:T(4,128)} %copy-done.4) | copy-start | bytes 2304004
  191.8 5.9 %copy-start.6 = (f32[8,2,4,3000]{3,2,1,0:T(4,128)S(1)}, f32[8,2,4,3000]{3,2,1,0:T(4,128)}, u32[]{:S(2)}) copy-start(f32[8,2,4,3000]{3,2,1,0:T(4,128)} %reshape.55) | copy-start | bytes 2304004
  191.8 5.9 %collective-permute-start.36 = (bf16[8,4,3000]{2,1,0:T(4,128)(2,1)S(1)}, bf16[8,4,3000]{2,1,0:T(4,128)(2,1)}, u32[]{:S(2)}, u32[]{:S(2)}) collective-permute-start(bf16[8,4,3000]{2,1,0:T(4,128)(2,1)S(1)} %fusion.104), channel_id=1, source_target_pairs={{0,8},{1,9},{2,10},{3,11},{4,12},{5,13},{6,14},{7,15},{8,0},{9,1},... | collective-permute-start | bytes 576008 | tf_op jit(solution)/shard_map/ppermute | solution.py:163
  (4 other events, 9.7 us)

commit v2 on v0

v2 whole, which is shorter than its diff:
```python
import jax
import jax.numpy as jnp
from jax import lax
from jax.experimental import pallas as pl
from jax.experimental.layout import Layout, with_layout_constraint
from jax.experimental.pallas import tpu as pltpu
from jax.sharding import PartitionSpec as P

NY, NH, NL, NZ, NC = 4, 2, 2, 4, 2
PARTS = (4, 4, 4)
SCALE = 16.0
TILE = 512

SWAP_H = [(i, i ^ 1) for i in range(NY * NH)]
SWAP_CORE = [(i, i ^ 1) for i in range(NL * NZ * NC)]
SWAP_L = [(i, i ^ (NZ * NC)) for i in range(NL * NZ * NC)]


def swap(x, axis, turn):
    n_aux = NL * NZ * NC
    pairs = []
    for i in range(NY * NH * n_aux):
        y, h, l, z, k = i // n_aux // NH, i // n_aux % NH, i % n_aux // (NZ * NC), i // NC % NZ, i % NC
        mask = 1 if k == turn else 3
        y, z = (y ^ mask, z) if axis == "y" else (y, z ^ mask)
        pairs.append((i, (y * NH + h) * n_aux + (l * NZ + z) * NC + k))
    return permuted(x, ("basis", "aux"), pairs)


def mask_of(slot, core):
    return jnp.where(slot == 0, 2, jnp.where(slot == 1, 1 + 2 * core, jnp.where(slot == 2, 3 - 2 * core, 0)))


def places():
    basis, aux = lax.axis_index("basis"), lax.axis_index("aux")
    return basis // NH, aux // (NZ * NC), aux // NC % NZ, aux % NC


def after(x, earlier):
    return lax.optimization_barrier((x, earlier))[0]


def by_rows(x):
    return with_layout_constraint(x, Layout(major_to_minor=tuple(range(x.ndim))))


def permuted(x, axis, pairs):
    return by_rows(lax.ppermute(by_rows(x), axis, pairs))


def f32(x):
    return x.astype(jnp.float32)


def b16(x):
    return x.astype(jnp.bfloat16)


def picked(virt_coeffs, quarter, start, rows):
    y, l, z, k = places()
    n_vir = virt_coeffs.shape[1]
    size = NY * NC * NZ * NL * rows
    at = lax.broadcasted_iota(jnp.int32, (n_vir, size), 1)
    r, at = at % rows, at // rows
    ll, at = at % NL, at // NL
    zz, at = at % NZ, at // NZ
    kk, yy = at % NC, at // NC
    core = k ^ kk
    place = ((l ^ (1 - ll)) * NZ + (z ^ mask_of(zz, core))) * NC + core
    column = (place * NY + (y ^ mask_of(yy, k))) * quarter + start + r
    pick = b16(lax.broadcasted_iota(jnp.int32, (n_vir, size), 0) == column)
    return b16(jnp.dot(virt_coeffs, pick, preferred_element_type=jnp.float32))


def placed_rows(done, quarter, start, rows, n_occ):
    y, _, _, k = places()
    size = NY * n_occ * rows
    shape = (NY * quarter * n_occ, size)
    at = lax.broadcasted_iota(jnp.int32, shape, 1)
    r, at = at % rows, at // rows
    i, yy = at % n_occ, at // n_occ
    row = ((y ^ mask_of(NY - 1 - yy, k)) * quarter + start + r) * n_occ + i
    place = f32(lax.broadcasted_iota(jnp.int32, shape, 0) == row)
    return jnp.dot(place, done, precision=lax.Precision.HIGHEST, preferred_element_type=jnp.float32)


def partial_sums(half_ints, cols):
    blocks = []
    for half in half_ints:
        block = lax.dot_general(cols, half, (((0,), (0,)), ((), ())), preferred_element_type=jnp.float32)
        blocks.append(by_rows((block * SCALE).astype(jnp.float16)))
    n_rows, width = blocks[0].shape
    halves = [block.reshape(2, 2, n_rows // NY, width) for block in blocks]
    return by_rows(jnp.stack([half[0] for half in halves])), by_rows(jnp.stack([half[1] for half in halves]))


def swapped_factor(factor):
    return lax.ppermute(factor, "aux", SWAP_CORE)


def fit_kernel(near, far, own, other, away, keep, rows):
    n_unit, n_occ, _, r, _ = near.shape

    @pl.when(pl.program_id(0) == 0)
    def _():
        for n, units in enumerate((near, far)):
            for u in range(n_unit):
                for i in range(n_occ):
                    g = (n * n_unit + u) * n_occ + i
                    for h in range(2):
                        rows[h, g * r : (g + 1) * r, :] = units[u, i, h]

    by_columns = (((1,), (1,)), ((), ()))
    total = lax.dot_general(rows[0], own[...], by_columns, preferred_element_type=jnp.float32)
    total = total + lax.dot_general(rows[1], other[...], by_columns, preferred_element_type=jnp.float32)
    one = r // (NZ * NL)
    for z in range(NZ):
        out = away if z < NZ // 2 else keep
        first = [g * r + (z * NL + l) * one for l in range(NL) for g in range(NY * n_occ)]
        out[0, z % (NZ // 2)] = jnp.concatenate([total[f : f + one] for f in first], 0).astype(out.dtype)


def fit(near, far, own, other):
    n_unit, n_occ, _, r, width = near.shape
    n_cols = own.shape[0]
    n_rows = 2 * n_unit * n_occ * r
    units = pl.BlockSpec(near.shape, lambda q: (0, 0, 0, 0, 0))
    factor = pl.BlockSpec((TILE, width), lambda q: (q, 0))
    out = pl.BlockSpec((1, NZ // 2, n_rows // NZ, TILE), lambda q: (0, 0, 0, q))
    shape = lambda d: jax.ShapeDtypeStruct((1, NZ // 2, n_rows // NZ, n_cols), d)
    return pl.pallas_call(
        fit_kernel,
        grid=(pl.cdiv(n_cols, TILE),),
        in_specs=[units] * 2 + [factor] * 2,
        out_specs=[out] * 2,
        out_shape=[shape(jnp.bfloat16), shape(jnp.float32)],
        scratch_shapes=[pltpu.VMEM((2, n_rows, width), jnp.bfloat16)],
        compiler_params=pltpu.CompilerParams(vmem_limit_bytes=40 << 20),
        cost_estimate=pl.CostEstimate(
            flops=4 * n_rows * width * n_cols,
            bytes_accessed=4 * width * n_cols + 3 * n_rows * n_cols,
            transcendentals=0,
        ),
    )(near, far, own, other)


class Part:
    def __init__(self, away, keep):
        self.away, self.keep = away, keep

    def sum_y(self, *ready):
        got = swap(after(self.away, ready), "y", 0)
        self.kept = f32(self.keep) + f32(got)

    def sum_y_again(self, *ready):
        got = swap(self.kept[:, 0].astype(jnp.float16), "y", 1)
        self.total = after(self.kept[:, 1], ready) + f32(got)

    def sum_h(self, *ready):
        got = permuted(self.total.astype(jnp.float16), "basis", SWAP_H)
        pair = b16((after(self.total, ready) + f32(got)) * (1 / SCALE))
        middle = pair.shape[1] // NC
        got = permuted(pair[:, middle:], "aux", SWAP_CORE)
        self.block = by_rows(jnp.stack([pair[:, :middle], got], axis=1))

    def gather_y(self, *ready):
        got = swap(self.block, "y", 1)
        self.near = by_rows(jnp.stack([after(self.block, ready), got]))

    def gather_y_again(self):
        self.far = swap(self.near, "y", 0)

    def fit(self, own, other, *ready):
        self.away, self.keep = fit(after(self.near, ready), self.far, own, other)

    def sum_z(self, *ready):
        got = swap(self.away, "z", 0)
        self.kept = after(self.keep, ready) + f32(got)

    def sum_z_again(self, *ready):
        got = swap(b16(self.kept[:, 0]), "z", 1)
        self.total = (after(self.kept[:, 1], ready) + f32(got))[0]

    def sum_l(self, *ready):
        middle = self.total.shape[0] // NL
        got = permuted(b16(self.total[:middle]), "aux", SWAP_L)
        self.done = after(self.total[middle:], ready) + f32(got)


def on_device(half_ints, virt_coeffs, metric_factor):
    n_occ = half_ints.shape[0]
    n_vir = virt_coeffs.shape[1]
    quarter = n_vir // (NL * NZ * NC * NY)
    starts = [sum(PARTS[:p]) for p in range(len(PARTS))]
    parts = range(len(PARTS))
    first, second, third = [
        Part(*partial_sums(half_ints, picked(virt_coeffs, quarter, starts[p], PARTS[p]))) for p in parts
    ]
    other = swapped_factor(metric_factor).T
    own = metric_factor.T
    first.sum_y()
    second.sum_y(first.kept)
    third.sum_y(second.kept)
    for part in (first, second, third):
        part.sum_y_again()
    first.sum_h()
    second.sum_h(third.kept, first.block)
    third.sum_h()
    first.gather_y()
    second.gather_y()
    for part in (first, second):
        part.gather_y_again()
    first.fit(own, other)
    third.gather_y(first.keep)
    third.gather_y_again()
    second.fit(own, other, third.near)
    third.fit(own, other)
    for part in (first, second, third):
        part.sum_z()
        part.sum_z_again()
        part.sum_l()
    done = [
        placed_rows(part.done, quarter, starts[p], PARTS[p], n_occ) for p, part in enumerate((first, second, third))
    ]
    return sum(done[1:], done[0])


def solution(mesh):
    placed = (P(None, "basis", "aux"), P("basis", None), P("aux", "basis"))
    return jax.shard_map(
        on_device, mesh=mesh, in_specs=placed, out_specs=P("aux", "basis"), check_vma=False
    )
```

time: 554 us -> 170 us (0.31)
  blocking collectives: 371 us -> 0 us
  starting transfers between devices: 0.01 us -> 36.6 us
  Pallas kernels: 0 us -> 25.9 us
  waiting for transfers between devices: 107 us -> 83.8 us
  local copies, waits for them, and re-layouts: 28.6 us -> 8.38 us
  matrix products: 29.1 us -> 11.1 us
  between operations: 13.4 us -> 0.65 us
    psum x1 -> x0, blocking collectives: 371 us -> none  [on_device(): pair_ints = lax.psum(partial_ints, 'basis').astype(jnp.bfloat16)]
    reduce_scatter x1 -> x0, waiting for transfers between devices: 107 us -> none  [on_device(): lax.psum_scatter(metric_apply(pair_ints, metric_factor), 'aux', scatter_d...]
    ppermute x0 -> x28, waiting for transfers between devices: none -> 83.8 us  [the longest x27 83.7 us: permuted(): return by_rows(lax.ppermute(by_rows(x), axis, pairs))]
    ppermute x0 -> x28, starting transfers between devices: none -> 36.6 us  [the longest x27 35.6 us: permuted(): return by_rows(lax.ppermute(by_rows(x), axis, pairs))]
    pallas_call x0 -> x3, Pallas kernels: none -> 25.9 us  [fit(): pl.pallas_call(fit_kernel, grid=(pl.cdiv(n_cols, TILE),), in_specs=[units...]
    dot_general x3 -> x12, matrix products: 29.1 us -> 11.1 us  [the longest x6 6.16 us: partial_sums(): lax.dot_general(cols, half, (((0,), (0,)), ((), ())), preferred_element_t...]
    another operation x1 -> x5, local copies, waits for them, and re-layouts: 14.9 us -> 0.14 us  [sum_h(): self.block = by_rows(jnp.stack([pair[:, :middle], got], axis=1))]
    reshape x1 -> x0, local copies, waits for them, and re-layouts: 12.3 us -> none  [on_device(): partial_ints = jnp.stack(blocks, axis=1).reshape(n_vir * n_occ, width)]
  transfers between devices with their start and end apart: 1 -> 28, of which waited for: 1 -> 14; matrix products, arithmetic and copies ran while one was open for 0% -> 7% of each run, Pallas kernels for 0% -> 10%
where the time goes in v2:
time: 170 us
  waiting for transfers between devices  83.8 us (49%)
  starting transfers between devices  36.6 us (22%)
  Pallas kernels  25.9 us (15%)
  matrix products  11.1 us (7%)
  local copies, waits for them, and re-layouts  8.38 us (5%)
  other arithmetic  3.48 us (2%)
    ppermute x27, waiting for transfers between devices, permuted(): return by_rows(lax.ppermute(by_rows(x), axis, pairs))  83.7 us
    ppermute x27, starting transfers between devices, permuted(): return by_rows(lax.ppermute(by_rows(x), axis, pairs))  35.6 us
    pallas_call x3, Pallas kernels, fit(): pl.pallas_call(fit_kernel, grid=(pl.cdiv(n_cols, TILE),), in_specs=[units...  25.9 us
    unnamed x20, local copies, waits for them, and re-layouts  7.02 us
    dot_general x6, matrix products, partial_sums(): lax.dot_general(cols, half, (((0,), (0,)), ((), ())), preferred_element_t...  6.16 us
  transfers between devices with their start and end apart: 28, of which 14 were waited for; matrix products, arithmetic and copies ran while one was open for 7% of the time, Pallas kernels for 10%

profile of v2, /device:TPU:0, one launch (start us, length us, event | category | flops | bytes accessed | tf_op | source)
XLA Modules:
  0.0 169.9 jit_solution(11325006923874067834)
XLA Ops:
  0.1 1.3 copy-done
  1.4 0.7 convolution_convert_fusion.2
  2.1 2.1 %copy-done.3 = bf16[2,1000,1500]{2,1,0:T(8,128)(2,1)S(1)} copy-done((bf16[2,1000,1500]{2,1,0:T(8,128)(2,1)S(1)}, bf16[2,1000,1500]{2,1,0:T(8,128)(2,1)}, u32[]{:S(2)}) %copy-start.3) | copy-done | bytes 6000024
  4.1 1.0 fusion.37
  5.2 1.0 fusion.46
  6.7 1.7 %collective-permute-start = (f16[2,2,64,1500]{3,2,1,0:T(8,128)(2,1)S(1)}, f16[2,2,64,1500]{3,2,1,0:T(8,128)(2,1)S(1)}, u32[]{:S(2)}, u32[]{:S(2)}) collective-permute-start(f16[2,2,64,1500]{3,2,1,0:T(8,128)(2,1)S(1)} %pad_maximum_fusion.1), channel_id=1, source_target_pairs={{0,32},{1,97},{2,34},{3,99},{4,36},{5,101},{6,38},{7,103},{8,40},{... | collective-permute-start | bytes 2304008 | tf_op jit(solution)/shard_map/ppermute | solution.py:48
  8.5 1.1 collective-permute-start.6
  9.5 0.7 convolution_convert_fusion
  10.2 0.7 convolution_convert_fusion.1
  10.9 1.0 fusion.34
  11.9 1.0 fusion.43
  13.2 1.0 fusion.31
  14.2 1.0 fusion.40
  15.6 3.2 %collective-permute-done = f16[2,2,64,1500]{3,2,1,0:T(8,128)(2,1)S(1)} collective-permute-done((f16[2,2,64,1500]{3,2,1,0:T(8,128)(2,1)S(1)}, f16[2,2,64,1500]{3,2,1,0:T(8,128)(2,1)S(1)}, u32[]{:S(2)}, u32[]{:S(2)}) %collective-permute-start) | collective-permute-done | bytes 768032 | tf_op jit(solution)/shard_map/ppermute | solution.py:48
  19.0 1.7 %collective-permute-start.10 = (f16[2,2,64,1500]{3,2,1,0:T(8,128)(2,1)S(1)}, f16[2,2,64,1500]{3,2,1,0:T(8,128)(2,1)S(1)}, u32[]{:S(2)}, u32[]{:S(2)}) collective-permute-start(f16[2,2,64,1500]{3,2,1,0:T(8,128)(2,1)S(1)} %pad_maximum_fusion.4), channel_id=1, source_target_pairs={{0,32},{1,97},{2,34},{3,99},{4,36},{5,101},{6,38},{7,103},{8,40},{... | collective-permute-start | bytes 2304008 | tf_op jit(solution)/shard_map/ppermute | solution.py:48
  20.9 2.3 %collective-permute-start.1 = (f16[2,64,1500]{2,1,0:T(8,128)(2,1)S(1)}, f16[2,64,1500]{2,1,0:T(8,128)(2,1)S(1)}, u32[]{:S(2)}, u32[]{:S(2)}) collective-permute-start(f16[2,64,1500]{2,1,0:T(8,128)(2,1)S(1)} %get-tuple-element.35), channel_id=1, source_target_pairs={{0,96},{1,33},{2,98},{3,35},{4,100},{5,37},{6,102},{7,39},{8,104},... | collective-permute-start | bytes 1152008 | tf_op jit(solution)/shard_map/ppermute | solution.py:48
  23.3 11.0 %collective-permute-done.1 = f16[2,64,1500]{2,1,0:T(8,128)(2,1)S(1)} collective-permute-done((f16[2,64,1500]{2,1,0:T(8,128)(2,1)S(1)}, f16[2,64,1500]{2,1,0:T(8,128)(2,1)S(1)}, u32[]{:S(2)}, u32[]{:S(2)}) %collective-permute-start.1) | collective-permute-done | bytes 384032 | tf_op jit(solution)/shard_map/ppermute | solution.py:48
  34.4 3.1 %collective-permute-start.2 = (f16[2,64,1500]{2,1,0:T(8,128)(2,1)S(1)}, f16[2,64,1500]{2,1,0:T(8,128)(2,1)S(1)}, u32[]{:S(2)}, u32[]{:S(2)}) collective-permute-start(f16[2,64,1500]{2,1,0:T(8,128)(2,1)S(1)} %get-tuple-element.29), channel_id=1, source_target_pairs={{0,16},{16,0},{32,48},{48,32},{64,80},{80,64},{96,112},{112,96},{1... | collective-permute-start | bytes 1152008 | tf_op jit(solution)/shard_map/ppermute | solution.py:48
  37.8 2.3 %collective-permute-start.11 = (f16[2,64,1500]{2,1,0:T(8,128)(2,1)S(1)}, f16[2,64,1500]{2,1,0:T(8,128)(2,1)S(1)}, u32[]{:S(2)}, u32[]{:S(2)}) collective-permute-start(f16[2,64,1500]{2,1,0:T(8,128)(2,1)S(1)} %get-tuple-element.33), channel_id=1, source_target_pairs={{0,96},{1,33},{2,98},{3,35},{4,100},{5,37},{6,102},{7,39},{8,104},... | collective-permute-start | bytes 1152008 | tf_op jit(solution)/shard_map/ppermute | solution.py:48
  40.1 5.9 %collective-permute-done.2 = f16[2,64,1500]{2,1,0:T(8,128)(2,1)S(1)} collective-permute-done((f16[2,64,1500]{2,1,0:T(8,128)(2,1)S(1)}, f16[2,64,1500]{2,1,0:T(8,128)(2,1)S(1)}, u32[]{:S(2)}, u32[]{:S(2)}) %collective-permute-start.2) | collective-permute-done | bytes 384032 | tf_op jit(solution)/shard_map/ppermute | solution.py:48
  46.6 1.0 collective-permute-done.3
  47.9 3.3 %collective-permute-start.13 = (f16[2,64,1500]{2,1,0:T(8,128)(2,1)S(1)}, f16[2,64,1500]{2,1,0:T(8,128)(2,1)S(1)}, u32[]{:S(2)}, u32[]{:S(2)}) collective-permute-start(f16[2,64,1500]{2,1,0:T(8,128)(2,1)S(1)} %get-tuple-element.27), channel_id=1, source_target_pairs={{0,16},{16,0},{32,48},{48,32},{64,80},{80,64},{96,112},{112,96},{1... | collective-permute-start | bytes 1152008 | tf_op jit(solution)/shard_map/ppermute | solution.py:48
  51.2 11.4 %collective-permute-done.12 = f16[2,2,64,1500]{3,2,1,0:T(8,128)(2,1)S(1)} collective-permute-done((f16[2,2,64,1500]{3,2,1,0:T(8,128)(2,1)S(1)}, f16[2,2,64,1500]{3,2,1,0:T(8,128)(2,1)S(1)}, u32[]{:S(2)}, u32[]{:S(2)}) %collective-permute-start.12) | collective-permute-done | bytes 768032 | tf_op jit(solution)/shard_map/ppermute | solution.py:48
  63.3 0.6 collective-permute-start.14
  64.0 8.2 %collective-permute-done.16 = f16[2,64,1500]{2,1,0:T(8,128)(2,1)S(1)} collective-permute-done((f16[2,64,1500]{2,1,0:T(8,128)(2,1)S(1)}, f16[2,64,1500]{2,1,0:T(8,128)(2,1)S(1)}, u32[]{:S(2)}, u32[]{:S(2)}) %collective-permute-start.16) | collective-permute-done | bytes 384032 | tf_op jit(solution)/shard_map/ppermute | solution.py:48
  72.3 3.1 %collective-permute-start.17 = (f16[2,64,1500]{2,1,0:T(8,128)(2,1)S(1)}, f16[2,64,1500]{2,1,0:T(8,128)(2,1)S(1)}, u32[]{:S(2)}, u32[]{:S(2)}) collective-permute-start(f16[2,64,1500]{2,1,0:T(8,128)(2,1)S(1)} %get-tuple-element.31), channel_id=1, source_target_pairs={{0,16},{16,0},{32,48},{48,32},{64,80},{80,64},{96,112},{112,96},{1... | collective-permute-start | bytes 1152008 | tf_op jit(solution)/shard_map/ppermute | solution.py:48
  75.7 7.6 %collective-permute-done.17 = f16[2,64,1500]{2,1,0:T(8,128)(2,1)S(1)} collective-permute-done((f16[2,64,1500]{2,1,0:T(8,128)(2,1)S(1)}, f16[2,64,1500]{2,1,0:T(8,128)(2,1)S(1)}, u32[]{:S(2)}, u32[]{:S(2)}) %collective-permute-start.17) | collective-permute-done | bytes 384032 | tf_op jit(solution)/shard_map/ppermute | solution.py:48
  83.6 5.4 %collective-permute-done.15 = bf16[2,2,32,1500]{3,2,1,0:T(8,128)(2,1)S(1)} collective-permute-done((bf16[2,2,32,1500]{3,2,1,0:T(8,128)(2,1)S(1)}, bf16[2,2,32,1500]{3,2,1,0:T(8,128)(2,1)S(1)}, u32[]{:S(2)}, u32[]{:S(2)}) %collective-permute-start.15) | collective-permute-done | bytes 384032 | tf_op jit(solution)/shard_map/ppermute | solution.py:48
  89.1 0.9 collective-permute-start.20
  90.4 3.6 %copy-done.2 = bf16[1500,3000]{0,1:T(8,128)(2,1)} copy-done((bf16[1500,3000]{0,1:T(8,128)(2,1)}, bf16[1500,3000]{0,1:T(8,128)(2,1)S(1)}, u32[]{:S(2)}) %copy-start.2) | copy-done | bytes 9000024
  94.0 8.6 %shard_map.37 = (bf16[1,2,64,3000]{3,2,1,0:T(8,128)(2,1)S(1)}, f32[1,2,64,3000]{3,2,1,0:T(8,128)S(1)}) custom-call(bf16[2,2,2,32,1500]{4,3,2,1,0:T(8,128)(2,1)S(1)} %pad_maximum_fusion.2.near, bf16[2,2,2,32,1500]{4,3,2,1,0:T(8,128)(2,1)S(1)} %collective-permute-done.5.far, bf16[3000,1500]{1,0:T(8,128)(2,1)S(1)} %bitcast.116, bf16[3000,1500]{1,0:T(8,128)(2,1)} %bitcast.119), custom_call_target="tpu_custom_call" | custom-call | flops 4608000000 | bytes 20304000 | tf_op jit(solution)/shard_map/pallas_call | solution.py:131
  103.1 8.6 %shard_map.38 = (bf16[1,2,64,3000]{3,2,1,0:T(8,128)(2,1)S(1)}, f32[1,2,64,3000]{3,2,1,0:T(8,128)S(1)}) custom-call(bf16[2,2,2,32,1500]{4,3,2,1,0:T(8,128)(2,1)S(1)} %pad_maximum_fusion.7.near, bf16[2,2,2,32,1500]{4,3,2,1,0:T(8,128)(2,1)S(1)} %collective-permute-done.20.far, bf16[3000,1500]{1,0:T(8,128)(2,1)S(1)} %bitcast.117, bf16[3000,1500]{1,0:T(8,128)(2,1)} %bitcast.120), custom_call_target="tpu_custom_call" | custom-call | flops 4608000000 | bytes 20304000 | tf_op jit(solution)/shard_map/pallas_call | solution.py:131
  111.8 2.0 %collective-permute-start.21 = (bf16[1,2,64,3000]{3,2,1,0:T(8,128)(2,1)S(1)}, bf16[1,2,64,3000]{3,2,1,0:T(8,128)(2,1)S(1)}, u32[]{:S(2)}, u32[]{:S(2)}) collective-permute-start(bf16[1,2,64,3000]{3,2,1,0:T(8,128)(2,1)S(1)} %get-tuple-element.24), channel_id=1, source_target_pairs={{0,2},{1,7},{2,0},{3,5},{4,6},{5,3},{6,4},{7,1},{8,10},{9,15},{10,... | collective-permute-start | bytes 2304008 | tf_op jit(solution)/shard_map/ppermute | solution.py:48
  113.8 0.6 collective-permute-start.24
  114.5 9.3 %collective-permute-done.21 = bf16[1,2,64,3000]{3,2,1,0:T(8,128)(2,1)S(1)} collective-permute-done((bf16[1,2,64,3000]{3,2,1,0:T(8,128)(2,1)S(1)}, bf16[1,2,64,3000]{3,2,1,0:T(8,128)(2,1)S(1)}, u32[]{:S(2)}, u32[]{:S(2)}) %collective-permute-start.21) | collective-permute-done | bytes 768032 | tf_op jit(solution)/shard_map/ppermute | solution.py:48
  124.1 4.1 %collective-permute-start.22 = (bf16[1,64,3000]{2,1,0:T(8,128)(2,1)S(1)}, bf16[1,64,3000]{2,1,0:T(8,128)(2,1)S(1)}, u32[]{:S(2)}, u32[]{:S(2)}) collective-permute-start(bf16[1,64,3000]{2,1,0:T(8,128)(2,1)S(1)} %fusion.83), channel_id=1, source_target_pairs={{0,6},{1,3},{2,4},{3,1},{4,2},{5,7},{6,0},{7,5},{8,14},{9,11},{10,... | collective-permute-start | bytes 1152008 | tf_op jit(solution)/shard_map/ppermute | solution.py:48
  128.3 8.6 %shard_map.39 = (bf16[1,2,64,3000]{3,2,1,0:T(8,128)(2,1)S(1)}, f32[1,2,64,3000]{3,2,1,0:T(8,128)S(1)}) custom-call(bf16[2,2,2,32,1500]{4,3,2,1,0:T(8,128)(2,1)S(1)} %pad_maximum_fusion.8.near, bf16[2,2,2,32,1500]{4,3,2,1,0:T(8,128)(2,1)S(1)} %collective-permute-done.24.far, bf16[3000,1500]{1,0:T(8,128)(2,1)S(1)} %bitcast.118, bf16[3000,1500]{1,0:T(8,128)(2,1)} %bitcast.121), custom_call_target="tpu_custom_call" | custom-call | flops 4608000000 | bytes 20304000 | tf_op jit(solution)/shard_map/pallas_call | solution.py:131
  137.3 3.6 %collective-permute-start.8 = (bf16[1,64,3000]{2,1,0:T(8,128)(2,1)S(1)}, bf16[1,64,3000]{2,1,0:T(8,128)(2,1)S(1)}, u32[]{:S(2)}, u32[]{:S(2)}) collective-permute-start(bf16[1,64,3000]{2,1,0:T(8,128)(2,1)S(1)} %fusion.80), channel_id=1, source_target_pairs={{0,6},{1,3},{2,4},{3,1},{4,2},{5,7},{6,0},{7,5},{8,14},{9,11},{10,... | collective-permute-start | bytes 1152008 | tf_op jit(solution)/shard_map/ppermute | solution.py:48
  141.0 0.7 collective-permute-start.23
  141.7 9.2 %collective-permute-done.8 = bf16[1,64,3000]{2,1,0:T(8,128)(2,1)S(1)} collective-permute-done((bf16[1,64,3000]{2,1,0:T(8,128)(2,1)S(1)}, bf16[1,64,3000]{2,1,0:T(8,128)(2,1)S(1)}, u32[]{:S(2)}, u32[]{:S(2)}) %collective-permute-start.8) | collective-permute-done | bytes 384032 | tf_op jit(solution)/shard_map/ppermute | solution.py:48
  151.0 0.7 collective-permute-start.9
  151.7 0.6 fusion.88
  152.6 2.0 %collective-permute-start.26 = (bf16[1,64,3000]{2,1,0:T(8,128)(2,1)S(1)}, bf16[1,64,3000]{2,1,0:T(8,128)(2,1)S(1)}, u32[]{:S(2)}, u32[]{:S(2)}) collective-permute-start(bf16[1,64,3000]{2,1,0:T(8,128)(2,1)S(1)} %fusion.84), channel_id=1, source_target_pairs={{0,6},{1,3},{2,4},{3,1},{4,2},{5,7},{6,0},{7,5},{8,14},{9,11},{10,... | collective-permute-start | bytes 1152008 | tf_op jit(solution)/shard_map/ppermute | solution.py:48
  154.6 7.0 %collective-permute-done.26 = bf16[1,64,3000]{2,1,0:T(8,128)(2,1)S(1)} collective-permute-done((bf16[1,64,3000]{2,1,0:T(8,128)(2,1)S(1)}, bf16[1,64,3000]{2,1,0:T(8,128)(2,1)S(1)}, u32[]{:S(2)}, u32[]{:S(2)}) %collective-permute-start.26) | collective-permute-done | bytes 384032 | tf_op jit(solution)/shard_map/ppermute | solution.py:48
  161.8 1.5 collective-permute-start.27
  163.3 4.2 %collective-permute-done.27 = bf16[32,3000]{1,0:T(8,128)(2,1)S(1)} collective-permute-done((bf16[32,3000]{1,0:T(8,128)(2,1)S(1)}, bf16[32,3000]{1,0:T(8,128)(2,1)S(1)}, u32[]{:S(2)}, u32[]{:S(2)}) %collective-permute-start.27) | collective-permute-done | bytes 192032 | tf_op jit(solution)/shard_map/ppermute | solution.py:48
  167.5 0.6 fusion.85
  168.2 1.7 %fusion = f32[96,3000]{1,0:T(8,128)} fusion(f32[96,3000]{1,0:T(8,128)S(1)} %fusion.85, f32[96,3000]{1,0:T(8,128)S(1)} %fusion.88, f32[32,3000]{1,0:T(8,128)S(1)} %slice_bitcast_fusion.8, bf16[32,3000]{1,0:T(8,128)(2,1)S(1)} %collective-permute-done.9, s32[32]{0:T(128)S(1)} %get-tuple-element.66, s32[32]{0:T(128)S(1)} %get-tuple-element.67, ...), kind=kOutput, calls=%fused_computation.1 | convolution fusion | flops 111464448 | bytes 4032588 | tf_op jit(solution)/shard_map/dot_general | solution.py:84
  (101 shorter events, 6.7 us)
Async XLA Ops:
  0.0 1.4 copy-start
  1.4 2.7 %copy-start.3 = (bf16[2,1000,1500]{2,1,0:T(8,128)(2,1)S(1)}, bf16[2,1000,1500]{2,1,0:T(8,128)(2,1)}, u32[]{:S(2)}) copy-start(bf16[2,1000,1500]{2,1,0:T(8,128)(2,1)} %param.3) | copy-start | bytes 18000004
  4.1 4.3 %slice-start = ((s8[9216000]{0:T(1024)(128)(4,1)}), s8[4194304]{0:T(1024)(128)(4,1)S(1)}, s32[]{:S(2)}) async-start(s8[9216000]{0:T(1024)(128)(4,1)} %bitcast.112), calls=%async_computation | async-start | bytes 8388608
  4.1 4.3 %slice-start.1 = ((s8[9216000]{0:T(1024)(128)(4,1)}), s8[4194304]{0:T(1024)(128)(4,1)S(1)}, s32[]{:S(2)}) async-start(s8[9216000]{0:T(1024)(128)(4,1)} %bitcast.112), calls=%async_computation.1 | async-start | bytes 8388608
  5.2 3.3 %slice-start.2 = ((s8[9216000]{0:T(1024)(128)(4,1)}), s8[827392]{0:T(1024)(128)(4,1)S(1)}, s32[]{:S(2)}) async-start(s8[9216000]{0:T(1024)(128)(4,1)} %bitcast.112), calls=%async_computation.2 | async-start | bytes 1654784
  6.7 12.1 %collective-permute-start = (f16[2,2,64,1500]{3,2,1,0:T(8,128)(2,1)S(1)}, f16[2,2,64,1500]{3,2,1,0:T(8,128)(2,1)S(1)}, u32[]{:S(2)}, u32[]{:S(2)}) collective-permute-start(f16[2,2,64,1500]{3,2,1,0:T(8,128)(2,1)S(1)} %pad_maximum_fusion.1), channel_id=1, source_target_pairs={{0,32},{1,97},{2,34},{3,99},{4,36},{5,101},{6,38},{7,103},{8,40},{... | collective-permute-start | bytes 2304008 | tf_op jit(solution)/shard_map/ppermute | solution.py:48
  8.5 82.0 %collective-permute-start.6 = (bf16[1500,3000]{0,1:T(8,128)(2,1)S(1)}, bf16[1500,3000]{0,1:T(8,128)(2,1)S(1)}, u32[]{:S(2)}, u32[]{:S(2)}) collective-permute-start(bf16[1500,3000]{0,1:T(8,128)(2,1)S(1)} %bitcast.113), channel_id=1, source_target_pairs={{0,1},{1,0},{2,3},{3,2},{4,5},{5,4},{6,7},{7,6},{8,9},{9,8},{10,11... | collective-permute-start | bytes 27000008 | tf_op jit(solution)/shard_map/ppermute | solution.py:98
  19.0 18.4 %collective-permute-start.10 = (f16[2,2,64,1500]{3,2,1,0:T(8,128)(2,1)S(1)}, f16[2,2,64,1500]{3,2,1,0:T(8,128)(2,1)S(1)}, u32[]{:S(2)}, u32[]{:S(2)}) collective-permute-start(f16[2,2,64,1500]{3,2,1,0:T(8,128)(2,1)S(1)} %pad_maximum_fusion.4), channel_id=1, source_target_pairs={{0,32},{1,97},{2,34},{3,99},{4,36},{5,101},{6,38},{7,103},{8,40},{... | collective-permute-start | bytes 2304008 | tf_op jit(solution)/shard_map/ppermute | solution.py:48
  20.9 13.3 %collective-permute-start.1 = (f16[2,64,1500]{2,1,0:T(8,128)(2,1)S(1)}, f16[2,64,1500]{2,1,0:T(8,128)(2,1)S(1)}, u32[]{:S(2)}, u32[]{:S(2)}) collective-permute-start(f16[2,64,1500]{2,1,0:T(8,128)(2,1)S(1)} %get-tuple-element.35), channel_id=1, source_target_pairs={{0,96},{1,33},{2,98},{3,35},{4,100},{5,37},{6,102},{7,39},{8,104},... | collective-permute-start | bytes 1152008 | tf_op jit(solution)/shard_map/ppermute | solution.py:48
  34.4 11.6 %collective-permute-start.2 = (f16[2,64,1500]{2,1,0:T(8,128)(2,1)S(1)}, f16[2,64,1500]{2,1,0:T(8,128)(2,1)S(1)}, u32[]{:S(2)}, u32[]{:S(2)}) collective-permute-start(f16[2,64,1500]{2,1,0:T(8,128)(2,1)S(1)} %get-tuple-element.29), channel_id=1, source_target_pairs={{0,16},{16,0},{32,48},{48,32},{64,80},{80,64},{96,112},{112,96},{1... | collective-permute-start | bytes 1152008 | tf_op jit(solution)/shard_map/ppermute | solution.py:48
  37.8 10.0 %collective-permute-start.11 = (f16[2,64,1500]{2,1,0:T(8,128)(2,1)S(1)}, f16[2,64,1500]{2,1,0:T(8,128)(2,1)S(1)}, u32[]{:S(2)}, u32[]{:S(2)}) collective-permute-start(f16[2,64,1500]{2,1,0:T(8,128)(2,1)S(1)} %get-tuple-element.33), channel_id=1, source_target_pairs={{0,96},{1,33},{2,98},{3,35},{4,100},{5,37},{6,102},{7,39},{8,104},... | collective-permute-start | bytes 1152008 | tf_op jit(solution)/shard_map/ppermute | solution.py:48
  46.1 1.5 collective-permute-start.3
  46.4 16.3 %collective-permute-start.12 = (f16[2,2,64,1500]{3,2,1,0:T(8,128)(2,1)S(1)}, f16[2,2,64,1500]{3,2,1,0:T(8,128)(2,1)S(1)}, u32[]{:S(2)}, u32[]{:S(2)}) collective-permute-start(f16[2,2,64,1500]{3,2,1,0:T(8,128)(2,1)S(1)} %pad_maximum_fusion.6), channel_id=1, source_target_pairs={{0,32},{1,97},{2,34},{3,99},{4,36},{5,101},{6,38},{7,103},{8,40},{... | collective-permute-start | bytes 2304008 | tf_op jit(solution)/shard_map/ppermute | solution.py:48
  47.7 27.7 %collective-permute-start.4 = (bf16[2,2,32,1500]{3,2,1,0:T(8,128)(2,1)S(1)}, bf16[2,2,32,1500]{3,2,1,0:T(8,128)(2,1)S(1)}, u32[]{:S(2)}, u32[]{:S(2)}) collective-permute-start(bf16[2,2,32,1500]{3,2,1,0:T(8,128)(2,1)S(1)} %copy.6), channel_id=1, source_target_pairs={{0,96},{1,33},{2,98},{3,35},{4,100},{5,37},{6,102},{7,39},{8,104},... | collective-permute-start | bytes 1152008 | tf_op jit(solution)/shard_map/ppermute | solution.py:48
  47.8 46.2 %slice-start.3 = ((s8[9216000]{0:T(1024)(128)(4,1)}), s8[4194304]{0:T(1024)(128)(4,1)S(1)}, s32[]{:S(2)}) async-start(s8[9216000]{0:T(1024)(128)(4,1)} %bitcast.114), calls=%async_computation.3 | async-start | bytes 8388608
  47.9 15.2 %collective-permute-start.13 = (f16[2,64,1500]{2,1,0:T(8,128)(2,1)S(1)}, f16[2,64,1500]{2,1,0:T(8,128)(2,1)S(1)}, u32[]{:S(2)}, u32[]{:S(2)}) collective-permute-start(f16[2,64,1500]{2,1,0:T(8,128)(2,1)S(1)} %get-tuple-element.27), channel_id=1, source_target_pairs={{0,16},{16,0},{32,48},{48,32},{64,80},{80,64},{96,112},{112,96},{1... | collective-permute-start | bytes 1152008 | tf_op jit(solution)/shard_map/ppermute | solution.py:48
  62.9 31.1 %slice-start.4 = ((s8[9216000]{0:T(1024)(128)(4,1)}), s8[4194304]{0:T(1024)(128)(4,1)S(1)}, s32[]{:S(2)}) async-start(s8[9216000]{0:T(1024)(128)(4,1)} %bitcast.114), calls=%async_computation.4 | async-start | bytes 8388608
  63.1 9.1 %collective-permute-start.16 = (f16[2,64,1500]{2,1,0:T(8,128)(2,1)S(1)}, f16[2,64,1500]{2,1,0:T(8,128)(2,1)S(1)}, u32[]{:S(2)}, u32[]{:S(2)}) collective-permute-start(f16[2,64,1500]{2,1,0:T(8,128)(2,1)S(1)} %get-tuple-element.37), channel_id=1, source_target_pairs={{0,96},{1,33},{2,98},{3,35},{4,100},{5,37},{6,102},{7,39},{8,104},... | collective-permute-start | bytes 1152008 | tf_op jit(solution)/shard_map/ppermute | solution.py:48
  63.3 12.2 %collective-permute-start.14 = (bf16[2,32,1500]{2,1,0:T(8,128)(2,1)S(1)}, bf16[2,32,1500]{2,1,0:T(8,128)(2,1)S(1)}, u32[]{:S(2)}, u32[]{:S(2)}) collective-permute-start(bf16[2,32,1500]{2,1,0:T(8,128)(2,1)S(1)} %get-tuple-element.52), channel_id=1, source_target_pairs={{0,1},{1,0},{2,3},{3,2},{4,5},{5,4},{6,7},{7,6},{8,9},{9,8},{10,11... | collective-permute-start | bytes 576008 | tf_op jit(solution)/shard_map/ppermute | solution.py:48
  72.3 11.1 %collective-permute-start.17 = (f16[2,64,1500]{2,1,0:T(8,128)(2,1)S(1)}, f16[2,64,1500]{2,1,0:T(8,128)(2,1)S(1)}, u32[]{:S(2)}, u32[]{:S(2)}) collective-permute-start(f16[2,64,1500]{2,1,0:T(8,128)(2,1)S(1)} %get-tuple-element.31), channel_id=1, source_target_pairs={{0,16},{16,0},{32,48},{48,32},{64,80},{80,64},{96,112},{112,96},{1... | collective-permute-start | bytes 1152008 | tf_op jit(solution)/shard_map/ppermute | solution.py:48
  75.4 18.7 %slice-start.5 = ((s8[9216000]{0:T(1024)(128)(4,1)}), s8[827392]{0:T(1024)(128)(4,1)S(1)}, s32[]{:S(2)}) async-start(s8[9216000]{0:T(1024)(128)(4,1)} %bitcast.114), calls=%async_computation.5 | async-start | bytes 1654784
  75.5 15.0 %collective-permute-start.5 = (bf16[2,2,2,32,1500]{4,3,2,1,0:T(8,128)(2,1)S(1)}, bf16[2,2,2,32,1500]{4,3,2,1,0:T(8,128)(2,1)S(1)}, u32[]{:S(2)}, u32[]{:S(2)}) collective-permute-start(bf16[2,2,2,32,1500]{4,3,2,1,0:T(8,128)(2,1)S(1)} %pad_maximum_fusion.2.near), channel_id=1, source_target_pairs={{0,32},{1,97},{2,34},{3,99},{4,36},{5,101},{6,38},{7,103},{8,40},{... | collective-permute-start | bytes 2304008 | tf_op jit(solution)/shard_map/ppermute | solution.py:48
  75.6 13.3 %collective-permute-start.15 = (bf16[2,2,32,1500]{3,2,1,0:T(8,128)(2,1)S(1)}, bf16[2,2,32,1500]{3,2,1,0:T(8,128)(2,1)S(1)}, u32[]{:S(2)}, u32[]{:S(2)}) collective-permute-start(bf16[2,2,32,1500]{3,2,1,0:T(8,128)(2,1)S(1)} %copy.11), channel_id=1, source_target_pairs={{0,96},{1,33},{2,98},{3,35},{4,100},{5,37},{6,102},{7,39},{8,104},... | collective-permute-start | bytes 1152008 | tf_op jit(solution)/shard_map/ppermute | solution.py:48
  83.5 6.4 %collective-permute-start.18 = (bf16[2,32,1500]{2,1,0:T(8,128)(2,1)S(1)}, bf16[2,32,1500]{2,1,0:T(8,128)(2,1)S(1)}, u32[]{:S(2)}, u32[]{:S(2)}) collective-permute-start(bf16[2,32,1500]{2,1,0:T(8,128)(2,1)S(1)} %get-tuple-element.56), channel_id=1, source_target_pairs={{0,1},{1,0},{2,3},{3,2},{4,5},{5,4},{6,7},{7,6},{8,9},{9,8},{10,11... | collective-permute-start | bytes 576008 | tf_op jit(solution)/shard_map/ppermute | solution.py:48
  89.1 14.1 %collective-permute-start.20 = (bf16[2,2,2,32,1500]{4,3,2,1,0:T(8,128)(2,1)S(1)}, bf16[2,2,2,32,1500]{4,3,2,1,0:T(8,128)(2,1)S(1)}, u32[]{:S(2)}, u32[]{:S(2)}) collective-permute-start(bf16[2,2,2,32,1500]{4,3,2,1,0:T(8,128)(2,1)S(1)} %pad_maximum_fusion.7.near), channel_id=1, source_target_pairs={{0,32},{1,97},{2,34},{3,99},{4,36},{5,101},{6,38},{7,103},{8,40},{... | collective-permute-start | bytes 2304008 | tf_op jit(solution)/shard_map/ppermute | solution.py:48
  90.0 12.8 %collective-permute-start.19 = (bf16[2,2,32,1500]{3,2,1,0:T(8,128)(2,1)S(1)}, bf16[2,2,32,1500]{3,2,1,0:T(8,128)(2,1)S(1)}, u32[]{:S(2)}, u32[]{:S(2)}) collective-permute-start(bf16[2,2,32,1500]{3,2,1,0:T(8,128)(2,1)S(1)} %pad_maximum_fusion.11), channel_id=1, source_target_pairs={{0,96},{1,33},{2,98},{3,35},{4,100},{5,37},{6,102},{7,39},{8,104},... | collective-permute-start | bytes 1152008 | tf_op jit(solution)/shard_map/ppermute | solution.py:48
  90.4 3.6 %copy-start.2 = (bf16[1500,3000]{0,1:T(8,128)(2,1)}, bf16[1500,3000]{0,1:T(8,128)(2,1)S(1)}, u32[]{:S(2)}) copy-start(bf16[1500,3000]{0,1:T(8,128)(2,1)S(1)} %collective-permute-done.6) | copy-start | bytes 27000004
  111.8 12.1 %collective-permute-start.21 = (bf16[1,2,64,3000]{3,2,1,0:T(8,128)(2,1)S(1)}, bf16[1,2,64,3000]{3,2,1,0:T(8,128)(2,1)S(1)}, u32[]{:S(2)}, u32[]{:S(2)}) collective-permute-start(bf16[1,2,64,3000]{3,2,1,0:T(8,128)(2,1)S(1)} %get-tuple-element.24), channel_id=1, source_target_pairs={{0,2},{1,7},{2,0},{3,5},{4,6},{5,3},{6,4},{7,1},{8,10},{9,15},{10,... | collective-permute-start | bytes 2304008 | tf_op jit(solution)/shard_map/ppermute | solution.py:48
  113.8 14.5 %collective-permute-start.24 = (bf16[2,2,2,32,1500]{4,3,2,1,0:T(8,128)(2,1)S(1)}, bf16[2,2,2,32,1500]{4,3,2,1,0:T(8,128)(2,1)S(1)}, u32[]{:S(2)}, u32[]{:S(2)}) collective-permute-start(bf16[2,2,2,32,1500]{4,3,2,1,0:T(8,128)(2,1)S(1)} %pad_maximum_fusion.8.near), channel_id=1, source_target_pairs={{0,32},{1,97},{2,34},{3,99},{4,36},{5,101},{6,38},{7,103},{8,40},{... | collective-permute-start | bytes 2304008 | tf_op jit(solution)/shard_map/ppermute | solution.py:48
  114.4 22.6 %collective-permute-start.7 = (bf16[1,2,64,3000]{3,2,1,0:T(8,128)(2,1)S(1)}, bf16[1,2,64,3000]{3,2,1,0:T(8,128)(2,1)S(1)}, u32[]{:S(2)}, u32[]{:S(2)}) collective-permute-start(bf16[1,2,64,3000]{3,2,1,0:T(8,128)(2,1)S(1)} %get-tuple-element.17), channel_id=1, source_target_pairs={{0,2},{1,7},{2,0},{3,5},{4,6},{5,3},{6,4},{7,1},{8,10},{9,15},{10,... | collective-permute-start | bytes 2304008 | tf_op jit(solution)/shard_map/ppermute | solution.py:48
  124.1 16.7 %collective-permute-start.22 = (bf16[1,64,3000]{2,1,0:T(8,128)(2,1)S(1)}, bf16[1,64,3000]{2,1,0:T(8,128)(2,1)S(1)}, u32[]{:S(2)}, u32[]{:S(2)}) collective-permute-start(bf16[1,64,3000]{2,1,0:T(8,128)(2,1)S(1)} %fusion.83), channel_id=1, source_target_pairs={{0,6},{1,3},{2,4},{3,1},{4,2},{5,7},{6,0},{7,5},{8,14},{9,11},{10,... | collective-permute-start | bytes 1152008 | tf_op jit(solution)/shard_map/ppermute | solution.py:48
  136.9 15.5 %collective-permute-start.25 = (bf16[1,2,64,3000]{3,2,1,0:T(8,128)(2,1)S(1)}, bf16[1,2,64,3000]{3,2,1,0:T(8,128)(2,1)S(1)}, u32[]{:S(2)}, u32[]{:S(2)}) collective-permute-start(bf16[1,2,64,3000]{3,2,1,0:T(8,128)(2,1)S(1)} %get-tuple-element.26), channel_id=1, source_target_pairs={{0,2},{1,7},{2,0},{3,5},{4,6},{5,3},{6,4},{7,1},{8,10},{9,15},{10,... | collective-permute-start | bytes 2304008 | tf_op jit(solution)/shard_map/ppermute | solution.py:48
  137.3 13.6 %collective-permute-start.8 = (bf16[1,64,3000]{2,1,0:T(8,128)(2,1)S(1)}, bf16[1,64,3000]{2,1,0:T(8,128)(2,1)S(1)}, u32[]{:S(2)}, u32[]{:S(2)}) collective-permute-start(bf16[1,64,3000]{2,1,0:T(8,128)(2,1)S(1)} %fusion.80), channel_id=1, source_target_pairs={{0,6},{1,3},{2,4},{3,1},{4,2},{5,7},{6,0},{7,5},{8,14},{9,11},{10,... | collective-permute-start | bytes 1152008 | tf_op jit(solution)/shard_map/ppermute | solution.py:48
  141.0 10.7 %collective-permute-start.23 = (bf16[32,3000]{1,0:T(8,128)(2,1)S(1)}, bf16[32,3000]{1,0:T(8,128)(2,1)S(1)}, u32[]{:S(2)}, u32[]{:S(2)}) collective-permute-start(bf16[32,3000]{1,0:T(8,128)(2,1)S(1)} %fusion.108), channel_id=1, source_target_pairs={{0,8},{1,9},{2,10},{3,11},{4,12},{5,13},{6,14},{7,15},{8,0},{9,1},... | collective-permute-start | bytes 576008 | tf_op jit(solution)/shard_map/ppermute | solution.py:48
  151.0 17.1 %collective-permute-start.9 = (bf16[32,3000]{1,0:T(8,128)(2,1)S(1)}, bf16[32,3000]{1,0:T(8,128)(2,1)S(1)}, u32[]{:S(2)}, u32[]{:S(2)}) collective-permute-start(bf16[32,3000]{1,0:T(8,128)(2,1)S(1)} %fusion.107), channel_id=1, source_target_pairs={{0,8},{1,9},{2,10},{3,11},{4,12},{5,13},{6,14},{7,15},{8,0},{9,1},... | collective-permute-start | bytes 576008 | tf_op jit(solution)/shard_map/ppermute | solution.py:48
  152.6 9.1 %collective-permute-start.26 = (bf16[1,64,3000]{2,1,0:T(8,128)(2,1)S(1)}, bf16[1,64,3000]{2,1,0:T(8,128)(2,1)S(1)}, u32[]{:S(2)}, u32[]{:S(2)}) collective-permute-start(bf16[1,64,3000]{2,1,0:T(8,128)(2,1)S(1)} %fusion.84), channel_id=1, source_target_pairs={{0,6},{1,3},{2,4},{3,1},{4,2},{5,7},{6,0},{7,5},{8,14},{9,11},{10,... | collective-permute-start | bytes 1152008 | tf_op jit(solution)/shard_map/ppermute | solution.py:48
  161.8 5.7 %collective-permute-start.27 = (bf16[32,3000]{1,0:T(8,128)(2,1)S(1)}, bf16[32,3000]{1,0:T(8,128)(2,1)S(1)}, u32[]{:S(2)}, u32[]{:S(2)}) collective-permute-start(bf16[32,3000]{1,0:T(8,128)(2,1)S(1)} %fusion.109), channel_id=1, source_target_pairs={{0,8},{1,9},{2,10},{3,11},{4,12},{5,13},{6,14},{7,15},{8,0},{9,1},... | collective-permute-start | bytes 576008 | tf_op jit(solution)/shard_map/ppermute | solution.py:48
  167.5 2.4 %copy-start.1 = (bf16[1000,768]{1,0:T(8,128)(2,1)S(1)}, bf16[1000,768]{1,0:T(8,128)(2,1)}, u32[]{:S(2)}) copy-start(bf16[1000,768]{1,0:T(8,128)(2,1)} %param.4) | copy-start | bytes 4608004

commit v3 on v2

--- a/solution.py
+++ b/solution.py
@@ -207,16 +207,18 @@
     second.sum_h(third.kept, first.block)
     third.sum_h()
     first.gather_y()
-    second.gather_y()
+    second.gather_y(other)
     for part in (first, second):
         part.gather_y_again()
     first.fit(own, other)
     third.gather_y(first.keep)
     third.gather_y_again()
-    second.fit(own, other, third.near)
+    second.fit(own, other)
     third.fit(own, other)
+    first.sum_z()
+    third.sum_z()
+    second.sum_z(third.kept)
     for part in (first, second, third):
-        part.sum_z()
         part.sum_z_again()
         part.sum_l()
     done = [

time: 170 us -> 163 us (0.959)
  waiting for transfers between devices: 83.8 us -> 70.3 us
  starting transfers between devices: 36.6 us -> 42.6 us
    ppermute x27, waiting for transfers between devices: 83.7 us -> 70.3 us  [permuted(): return by_rows(lax.ppermute(by_rows(x), axis, pairs))]
    ppermute x27, starting transfers between devices: 35.6 us -> 41.6 us  [permuted(): return by_rows(lax.ppermute(by_rows(x), axis, pairs))]
  transfers between devices with their start and end apart: 28 -> 28, of which waited for: 14 -> 14; matrix products, arithmetic and copies ran while one was open for 7% -> 7% of each run, Pallas kernels for 10% -> 16%
where the time goes in v3:
time: 163 us; the launch traced here: 162 us
  waiting for transfers between devices  70.3 us (43%)
  starting transfers between devices  42.6 us (26%)
  Pallas kernels  25.9 us (16%)
  matrix products  11 us (7%)
  local copies, waits for them, and re-layouts  8.39 us (5%)
  other arithmetic  3.45 us (2%)
    ppermute x27, waiting for transfers between devices, permuted(): return by_rows(lax.ppermute(by_rows(x), axis, pairs))  70.3 us
    ppermute x27, starting transfers between devices, permuted(): return by_rows(lax.ppermute(by_rows(x), axis, pairs))  41.6 us
    pallas_call x3, Pallas kernels, fit(): pl.pallas_call(fit_kernel, grid=(pl.cdiv(n_cols, TILE),), in_specs=[units...  25.9 us
    unnamed x20, local copies, waits for them, and re-layouts  7.02 us
    dot_general x6, matrix products, partial_sums(): lax.dot_general(cols, half, (((0,), (0,)), ((), ())), preferred_element_t...  6.04 us
  transfers between devices with their start and end apart: 28, of which 14 were waited for; matrix products, arithmetic and copies ran while one was open for 7% of the time, Pallas kernels for 16%

profile of v3, /device:TPU:0, one launch (start us, length us, event | category | flops | bytes accessed | tf_op | source)
XLA Modules:
  0.0 162.2 jit_solution(17045675238806075823)
XLA Ops:
  0.1 1.3 copy-done
  2.1 2.1 %copy-done.3 = bf16[2,1000,1500]{2,1,0:T(8,128)(2,1)S(1)} copy-done((bf16[2,1000,1500]{2,1,0:T(8,128)(2,1)S(1)}, bf16[2,1000,1500]{2,1,0:T(8,128)(2,1)}, u32[]{:S(2)}) %copy-start.3) | copy-done | bytes 6000024
  4.1 1.0 fusion.37
  5.2 1.0 fusion.46
  6.7 1.8 %collective-permute-start = (f16[2,2,64,1500]{3,2,1,0:T(8,128)(2,1)S(1)}, f16[2,2,64,1500]{3,2,1,0:T(8,128)(2,1)S(1)}, u32[]{:S(2)}, u32[]{:S(2)}) collective-permute-start(f16[2,2,64,1500]{3,2,1,0:T(8,128)(2,1)S(1)} %pad_maximum_fusion.1), channel_id=1, source_target_pairs={{0,32},{1,97},{2,34},{3,99},{4,36},{5,101},{6,38},{7,103},{8,40},{... | collective-permute-start | bytes 2304008 | tf_op jit(solution)/shard_map/ppermute | solution.py:48
  8.4 1.1 collective-permute-start.6
  9.5 0.7 convolution_convert_fusion
  10.1 0.7 convolution_convert_fusion.1
  10.8 1.0 fusion.34
  11.8 1.0 fusion.43
  13.1 1.0 fusion.31
  14.3 1.0 fusion.40
  15.4 3.3 %collective-permute-done = f16[2,2,64,1500]{3,2,1,0:T(8,128)(2,1)S(1)} collective-permute-done((f16[2,2,64,1500]{3,2,1,0:T(8,128)(2,1)S(1)}, f16[2,2,64,1500]{3,2,1,0:T(8,128)(2,1)S(1)}, u32[]{:S(2)}, u32[]{:S(2)}) %collective-permute-start) | collective-permute-done | bytes 768032 | tf_op jit(solution)/shard_map/ppermute | solution.py:48
  19.1 3.2 %collective-permute-start.1 = (f16[2,64,1500]{2,1,0:T(8,128)(2,1)S(1)}, f16[2,64,1500]{2,1,0:T(8,128)(2,1)S(1)}, u32[]{:S(2)}, u32[]{:S(2)}) collective-permute-start(f16[2,64,1500]{2,1,0:T(8,128)(2,1)S(1)} %get-tuple-element.37), channel_id=1, source_target_pairs={{0,96},{1,33},{2,98},{3,35},{4,100},{5,37},{6,102},{7,39},{8,104},... | collective-permute-start | bytes 1152008 | tf_op jit(solution)/shard_map/ppermute | solution.py:48
  22.9 9.5 %collective-permute-done.1 = f16[2,64,1500]{2,1,0:T(8,128)(2,1)S(1)} collective-permute-done((f16[2,64,1500]{2,1,0:T(8,128)(2,1)S(1)}, f16[2,64,1500]{2,1,0:T(8,128)(2,1)S(1)}, u32[]{:S(2)}, u32[]{:S(2)}) %collective-permute-start.1) | collective-permute-done | bytes 384032 | tf_op jit(solution)/shard_map/ppermute | solution.py:48
  32.5 3.1 %collective-permute-start.2 = (f16[2,64,1500]{2,1,0:T(8,128)(2,1)S(1)}, f16[2,64,1500]{2,1,0:T(8,128)(2,1)S(1)}, u32[]{:S(2)}, u32[]{:S(2)}) collective-permute-start(f16[2,64,1500]{2,1,0:T(8,128)(2,1)S(1)} %get-tuple-element.31), channel_id=1, source_target_pairs={{0,16},{16,0},{32,48},{48,32},{64,80},{80,64},{96,112},{112,96},{1... | collective-permute-start | bytes 1152008 | tf_op jit(solution)/shard_map/ppermute | solution.py:48
  36.4 5.5 %collective-permute-done.2 = f16[2,64,1500]{2,1,0:T(8,128)(2,1)S(1)} collective-permute-done((f16[2,64,1500]{2,1,0:T(8,128)(2,1)S(1)}, f16[2,64,1500]{2,1,0:T(8,128)(2,1)S(1)}, u32[]{:S(2)}, u32[]{:S(2)}) %collective-permute-start.2) | collective-permute-done | bytes 384032 | tf_op jit(solution)/shard_map/ppermute | solution.py:48
  42.2 3.1 %collective-permute-start.11 = (f16[2,64,1500]{2,1,0:T(8,128)(2,1)S(1)}, f16[2,64,1500]{2,1,0:T(8,128)(2,1)S(1)}, u32[]{:S(2)}, u32[]{:S(2)}) collective-permute-start(f16[2,64,1500]{2,1,0:T(8,128)(2,1)S(1)} %get-tuple-element.35), channel_id=1, source_target_pairs={{0,96},{1,33},{2,98},{3,35},{4,100},{5,37},{6,102},{7,39},{8,104},... | collective-permute-start | bytes 1152008 | tf_op jit(solution)/shard_map/ppermute | solution.py:48
  45.5 1.3 collective-permute-start.4
  46.8 3.6 %collective-permute-done.12 = f16[2,2,64,1500]{3,2,1,0:T(8,128)(2,1)S(1)} collective-permute-done((f16[2,2,64,1500]{3,2,1,0:T(8,128)(2,1)S(1)}, f16[2,2,64,1500]{3,2,1,0:T(8,128)(2,1)S(1)}, u32[]{:S(2)}, u32[]{:S(2)}) %collective-permute-start.12) | collective-permute-done | bytes 768032 | tf_op jit(solution)/shard_map/ppermute | solution.py:48
  50.8 3.3 %collective-permute-start.17 = (f16[2,64,1500]{2,1,0:T(8,128)(2,1)S(1)}, f16[2,64,1500]{2,1,0:T(8,128)(2,1)S(1)}, u32[]{:S(2)}, u32[]{:S(2)}) collective-permute-start(f16[2,64,1500]{2,1,0:T(8,128)(2,1)S(1)} %get-tuple-element.39), channel_id=1, source_target_pairs={{0,96},{1,33},{2,98},{3,35},{4,100},{5,37},{6,102},{7,39},{8,104},... | collective-permute-start | bytes 1152008 | tf_op jit(solution)/shard_map/ppermute | solution.py:48
  54.2 1.9 %collective-permute-start.13 = (f16[2,64,1500]{2,1,0:T(8,128)(2,1)S(1)}, f16[2,64,1500]{2,1,0:T(8,128)(2,1)S(1)}, u32[]{:S(2)}, u32[]{:S(2)}) collective-permute-start(f16[2,64,1500]{2,1,0:T(8,128)(2,1)S(1)} %get-tuple-element.29), channel_id=1, source_target_pairs={{0,16},{16,0},{32,48},{48,32},{64,80},{80,64},{96,112},{112,96},{1... | collective-permute-start | bytes 1152008 | tf_op jit(solution)/shard_map/ppermute | solution.py:48
  56.1 1.0 collective-permute-done.4
  57.3 4.7 %collective-permute-done.17 = f16[2,64,1500]{2,1,0:T(8,128)(2,1)S(1)} collective-permute-done((f16[2,64,1500]{2,1,0:T(8,128)(2,1)S(1)}, f16[2,64,1500]{2,1,0:T(8,128)(2,1)S(1)}, u32[]{:S(2)}, u32[]{:S(2)}) %collective-permute-start.17) | collective-permute-done | bytes 384032 | tf_op jit(solution)/shard_map/ppermute | solution.py:48
  62.1 4.3 %collective-permute-start.18 = (f16[2,64,1500]{2,1,0:T(8,128)(2,1)S(1)}, f16[2,64,1500]{2,1,0:T(8,128)(2,1)S(1)}, u32[]{:S(2)}, u32[]{:S(2)}) collective-permute-start(f16[2,64,1500]{2,1,0:T(8,128)(2,1)S(1)} %get-tuple-element.33), channel_id=1, source_target_pairs={{0,16},{16,0},{32,48},{48,32},{64,80},{80,64},{96,112},{112,96},{1... | collective-permute-start | bytes 1152008 | tf_op jit(solution)/shard_map/ppermute | solution.py:48
  66.5 7.0 %collective-permute-done.18 = f16[2,64,1500]{2,1,0:T(8,128)(2,1)S(1)} collective-permute-done((f16[2,64,1500]{2,1,0:T(8,128)(2,1)S(1)}, f16[2,64,1500]{2,1,0:T(8,128)(2,1)S(1)}, u32[]{:S(2)}, u32[]{:S(2)}) %collective-permute-start.18) | collective-permute-done | bytes 384032 | tf_op jit(solution)/shard_map/ppermute | solution.py:48
  74.3 0.8 collective-permute-done.19
  75.2 3.3 %collective-permute-start.20 = (bf16[2,2,32,1500]{3,2,1,0:T(8,128)(2,1)S(1)}, bf16[2,2,32,1500]{3,2,1,0:T(8,128)(2,1)S(1)}, u32[]{:S(2)}, u32[]{:S(2)}) collective-permute-start(bf16[2,2,32,1500]{3,2,1,0:T(8,128)(2,1)S(1)} %pad_maximum_fusion.11), channel_id=1, source_target_pairs={{0,96},{1,33},{2,98},{3,35},{4,100},{5,37},{6,102},{7,39},{8,104},... | collective-permute-start | bytes 1152008 | tf_op jit(solution)/shard_map/ppermute | solution.py:48
  78.4 3.6 %copy-done.2 = bf16[1500,3000]{0,1:T(8,128)(2,1)} copy-done((bf16[1500,3000]{0,1:T(8,128)(2,1)}, bf16[1500,3000]{0,1:T(8,128)(2,1)S(1)}, u32[]{:S(2)}) %copy-start.2) | copy-done | bytes 9000024
  82.0 8.6 %shard_map.37 = (bf16[1,2,64,3000]{3,2,1,0:T(8,128)(2,1)S(1)}, f32[1,2,64,3000]{3,2,1,0:T(8,128)S(1)}) custom-call(bf16[2,2,2,32,1500]{4,3,2,1,0:T(8,128)(2,1)S(1)} %pad_maximum_fusion.2.near, bf16[2,2,2,32,1500]{4,3,2,1,0:T(8,128)(2,1)S(1)} %collective-permute-done.5.far, bf16[3000,1500]{1,0:T(8,128)(2,1)S(1)} %bitcast.116, bf16[3000,1500]{1,0:T(8,128)(2,1)} %bitcast.119), custom_call_target="tpu_custom_call" | custom-call | flops 4608000000 | bytes 20304000 | tf_op jit(solution)/shard_map/pallas_call | solution.py:131
  91.1 2.0 %collective-permute-start.7 = (bf16[1,2,64,3000]{3,2,1,0:T(8,128)(2,1)S(1)}, bf16[1,2,64,3000]{3,2,1,0:T(8,128)(2,1)S(1)}, u32[]{:S(2)}, u32[]{:S(2)}) collective-permute-start(bf16[1,2,64,3000]{3,2,1,0:T(8,128)(2,1)S(1)} %get-tuple-element.18), channel_id=1, source_target_pairs={{0,2},{1,7},{2,0},{3,5},{4,6},{5,3},{6,4},{7,1},{8,10},{9,15},{10,... | collective-permute-start | bytes 2304008 | tf_op jit(solution)/shard_map/ppermute | solution.py:48
  93.1 11.2 %collective-permute-done.15 = bf16[2,2,32,1500]{3,2,1,0:T(8,128)(2,1)S(1)} collective-permute-done((bf16[2,2,32,1500]{3,2,1,0:T(8,128)(2,1)S(1)}, bf16[2,2,32,1500]{3,2,1,0:T(8,128)(2,1)S(1)}, u32[]{:S(2)}, u32[]{:S(2)}) %collective-permute-start.15) | collective-permute-done | bytes 384032 | tf_op jit(solution)/shard_map/ppermute | solution.py:48
  104.4 0.9 collective-permute-start.16
  105.2 0.9 collective-permute-done.21.far
  106.1 8.6 %shard_map.39 = (bf16[1,2,64,3000]{3,2,1,0:T(8,128)(2,1)S(1)}, f32[1,2,64,3000]{3,2,1,0:T(8,128)S(1)}) custom-call(bf16[2,2,2,32,1500]{4,3,2,1,0:T(8,128)(2,1)S(1)} %pad_maximum_fusion.8.near, bf16[2,2,2,32,1500]{4,3,2,1,0:T(8,128)(2,1)S(1)} %collective-permute-done.21.far, bf16[3000,1500]{1,0:T(8,128)(2,1)S(1)} %bitcast.117, bf16[3000,1500]{1,0:T(8,128)(2,1)} %bitcast.120), custom_call_target="tpu_custom_call" | custom-call | flops 4608000000 | bytes 20304000 | tf_op jit(solution)/shard_map/pallas_call | solution.py:131
  114.8 2.0 %collective-permute-start.22 = (bf16[1,2,64,3000]{3,2,1,0:T(8,128)(2,1)S(1)}, bf16[1,2,64,3000]{3,2,1,0:T(8,128)(2,1)S(1)}, u32[]{:S(2)}, u32[]{:S(2)}) collective-permute-start(bf16[1,2,64,3000]{3,2,1,0:T(8,128)(2,1)S(1)} %get-tuple-element.26), channel_id=1, source_target_pairs={{0,2},{1,7},{2,0},{3,5},{4,6},{5,3},{6,4},{7,1},{8,10},{9,15},{10,... | collective-permute-start | bytes 2304008 | tf_op jit(solution)/shard_map/ppermute | solution.py:48
  117.0 2.6 %collective-permute-start.8 = (bf16[1,64,3000]{2,1,0:T(8,128)(2,1)S(1)}, bf16[1,64,3000]{2,1,0:T(8,128)(2,1)S(1)}, u32[]{:S(2)}, u32[]{:S(2)}) collective-permute-start(bf16[1,64,3000]{2,1,0:T(8,128)(2,1)S(1)} %fusion.80), channel_id=1, source_target_pairs={{0,6},{1,3},{2,4},{3,1},{4,2},{5,7},{6,0},{7,5},{8,14},{9,11},{10,... | collective-permute-start | bytes 1152008 | tf_op jit(solution)/shard_map/ppermute | solution.py:48
  119.7 8.6 %shard_map.38 = (bf16[1,2,64,3000]{3,2,1,0:T(8,128)(2,1)S(1)}, f32[1,2,64,3000]{3,2,1,0:T(8,128)S(1)}) custom-call(bf16[2,2,2,32,1500]{4,3,2,1,0:T(8,128)(2,1)S(1)} %pad_maximum_fusion.7.near, bf16[2,2,2,32,1500]{4,3,2,1,0:T(8,128)(2,1)S(1)} %collective-permute-done.16.far, bf16[3000,1500]{1,0:T(8,128)(2,1)S(1)} %bitcast.118, bf16[3000,1500]{1,0:T(8,128)(2,1)} %bitcast.121), custom_call_target="tpu_custom_call" | custom-call | flops 4608000000 | bytes 20304000 | tf_op jit(solution)/shard_map/pallas_call | solution.py:131
  128.3 1.1 collective-permute-start.23
  129.4 1.0 collective-permute-done.8
  130.5 0.7 collective-permute-start.9
  131.4 2.6 %collective-permute-start.26 = (bf16[1,64,3000]{2,1,0:T(8,128)(2,1)S(1)}, bf16[1,64,3000]{2,1,0:T(8,128)(2,1)S(1)}, u32[]{:S(2)}, u32[]{:S(2)}) collective-permute-start(bf16[1,64,3000]{2,1,0:T(8,128)(2,1)S(1)} %fusion.84), channel_id=1, source_target_pairs={{0,6},{1,3},{2,4},{3,1},{4,2},{5,7},{6,0},{7,5},{8,14},{9,11},{10,... | collective-permute-start | bytes 1152008 | tf_op jit(solution)/shard_map/ppermute | solution.py:48
  134.1 10.5 %collective-permute-done.23 = bf16[1,2,64,3000]{3,2,1,0:T(8,128)(2,1)S(1)} collective-permute-done((bf16[1,2,64,3000]{3,2,1,0:T(8,128)(2,1)S(1)}, bf16[1,2,64,3000]{3,2,1,0:T(8,128)(2,1)S(1)}, u32[]{:S(2)}, u32[]{:S(2)}) %collective-permute-start.23) | collective-permute-done | bytes 768032 | tf_op jit(solution)/shard_map/ppermute | solution.py:48
  144.9 0.9 collective-permute-start.24
  145.9 1.3 collective-permute-start.27
  147.2 6.7 %collective-permute-done.24 = bf16[1,64,3000]{2,1,0:T(8,128)(2,1)S(1)} collective-permute-done((bf16[1,64,3000]{2,1,0:T(8,128)(2,1)S(1)}, bf16[1,64,3000]{2,1,0:T(8,128)(2,1)S(1)}, u32[]{:S(2)}, u32[]{:S(2)}) %collective-permute-start.24) | collective-permute-done | bytes 384032 | tf_op jit(solution)/shard_map/ppermute | solution.py:48
  155.4 4.5 %collective-permute-done.25 = bf16[32,3000]{1,0:T(8,128)(2,1)S(1)} collective-permute-done((bf16[32,3000]{1,0:T(8,128)(2,1)S(1)}, bf16[32,3000]{1,0:T(8,128)(2,1)S(1)}, u32[]{:S(2)}, u32[]{:S(2)}) %collective-permute-start.25) | collective-permute-done | bytes 192032 | tf_op jit(solution)/shard_map/ppermute | solution.py:48
  160.5 1.7 %fusion = f32[96,3000]{1,0:T(8,128)} fusion(f32[96,3000]{1,0:T(8,128)S(1)} %fusion.85, f32[96,3000]{1,0:T(8,128)S(1)} %fusion.88, f32[32,3000]{1,0:T(8,128)S(1)} %slice_bitcast_fusion.8, bf16[32,3000]{1,0:T(8,128)(2,1)S(1)} %collective-permute-done.9, s32[32]{0:T(128)S(1)} %get-tuple-element.68, s32[32]{0:T(128)S(1)} %get-tuple-element.69, ...), kind=kOutput, calls=%fused_computation.1 | convolution fusion | flops 111464448 | bytes 4032588 | tf_op jit(solution)/shard_map/dot_general | solution.py:84
  (101 shorter events, 9.2 us)
Async XLA Ops:
  0.0 1.4 copy-start
  1.4 2.7 %copy-start.3 = (bf16[2,1000,1500]{2,1,0:T(8,128)(2,1)S(1)}, bf16[2,1000,1500]{2,1,0:T(8,128)(2,1)}, u32[]{:S(2)}) copy-start(bf16[2,1000,1500]{2,1,0:T(8,128)(2,1)} %param.3) | copy-start | bytes 18000004
  4.1 4.3 %slice-start = ((s8[9216000]{0:T(1024)(128)(4,1)}), s8[4194304]{0:T(1024)(128)(4,1)S(1)}, s32[]{:S(2)}) async-start(s8[9216000]{0:T(1024)(128)(4,1)} %bitcast.112), calls=%async_computation | async-start | bytes 8388608
  4.1 4.3 %slice-start.1 = ((s8[9216000]{0:T(1024)(128)(4,1)}), s8[4194304]{0:T(1024)(128)(4,1)S(1)}, s32[]{:S(2)}) async-start(s8[9216000]{0:T(1024)(128)(4,1)} %bitcast.112), calls=%async_computation.1 | async-start | bytes 8388608
  5.2 3.3 %slice-start.2 = ((s8[9216000]{0:T(1024)(128)(4,1)}), s8[827392]{0:T(1024)(128)(4,1)S(1)}, s32[]{:S(2)}) async-start(s8[9216000]{0:T(1024)(128)(4,1)} %bitcast.112), calls=%async_computation.2 | async-start | bytes 1654784
  6.7 12.1 %collective-permute-start = (f16[2,2,64,1500]{3,2,1,0:T(8,128)(2,1)S(1)}, f16[2,2,64,1500]{3,2,1,0:T(8,128)(2,1)S(1)}, u32[]{:S(2)}, u32[]{:S(2)}) collective-permute-start(f16[2,2,64,1500]{3,2,1,0:T(8,128)(2,1)S(1)} %pad_maximum_fusion.1), channel_id=1, source_target_pairs={{0,32},{1,97},{2,34},{3,99},{4,36},{5,101},{6,38},{7,103},{8,40},{... | collective-permute-start | bytes 2304008 | tf_op jit(solution)/shard_map/ppermute | solution.py:48
  8.4 70.0 %collective-permute-start.6 = (bf16[1500,3000]{0,1:T(8,128)(2,1)S(1)}, bf16[1500,3000]{0,1:T(8,128)(2,1)S(1)}, u32[]{:S(2)}, u32[]{:S(2)}) collective-permute-start(bf16[1500,3000]{0,1:T(8,128)(2,1)S(1)} %bitcast.113), channel_id=1, source_target_pairs={{0,1},{1,0},{2,3},{3,2},{4,5},{5,4},{6,7},{7,6},{8,9},{9,8},{10,11... | collective-permute-start | bytes 27000008 | tf_op jit(solution)/shard_map/ppermute | solution.py:98
  19.1 13.3 %collective-permute-start.1 = (f16[2,64,1500]{2,1,0:T(8,128)(2,1)S(1)}, f16[2,64,1500]{2,1,0:T(8,128)(2,1)S(1)}, u32[]{:S(2)}, u32[]{:S(2)}) collective-permute-start(f16[2,64,1500]{2,1,0:T(8,128)(2,1)S(1)} %get-tuple-element.37), channel_id=1, source_target_pairs={{0,96},{1,33},{2,98},{3,35},{4,100},{5,37},{6,102},{7,39},{8,104},... | collective-permute-start | bytes 1152008 | tf_op jit(solution)/shard_map/ppermute | solution.py:48
  22.5 13.1 %collective-permute-start.10 = (f16[2,2,64,1500]{3,2,1,0:T(8,128)(2,1)S(1)}, f16[2,2,64,1500]{3,2,1,0:T(8,128)(2,1)S(1)}, u32[]{:S(2)}, u32[]{:S(2)}) collective-permute-start(f16[2,2,64,1500]{3,2,1,0:T(8,128)(2,1)S(1)} %pad_maximum_fusion.4), channel_id=1, source_target_pairs={{0,32},{1,97},{2,34},{3,99},{4,36},{5,101},{6,38},{7,103},{8,40},{... | collective-permute-start | bytes 2304008 | tf_op jit(solution)/shard_map/ppermute | solution.py:48
  32.5 9.4 %collective-permute-start.2 = (f16[2,64,1500]{2,1,0:T(8,128)(2,1)S(1)}, f16[2,64,1500]{2,1,0:T(8,128)(2,1)S(1)}, u32[]{:S(2)}, u32[]{:S(2)}) collective-permute-start(f16[2,64,1500]{2,1,0:T(8,128)(2,1)S(1)} %get-tuple-element.31), channel_id=1, source_target_pairs={{0,16},{16,0},{32,48},{48,32},{64,80},{80,64},{96,112},{112,96},{1... | collective-permute-start | bytes 1152008 | tf_op jit(solution)/shard_map/ppermute | solution.py:48
  35.9 14.5 %collective-permute-start.12 = (f16[2,2,64,1500]{3,2,1,0:T(8,128)(2,1)S(1)}, f16[2,2,64,1500]{3,2,1,0:T(8,128)(2,1)S(1)}, u32[]{:S(2)}, u32[]{:S(2)}) collective-permute-start(f16[2,2,64,1500]{3,2,1,0:T(8,128)(2,1)S(1)} %pad_maximum_fusion.6), channel_id=1, source_target_pairs={{0,32},{1,97},{2,34},{3,99},{4,36},{5,101},{6,38},{7,103},{8,40},{... | collective-permute-start | bytes 2304008 | tf_op jit(solution)/shard_map/ppermute | solution.py:48
  42.0 3.4 %collective-permute-start.3 = (bf16[2,32,1500]{2,1,0:T(8,128)(2,1)S(1)}, bf16[2,32,1500]{2,1,0:T(8,128)(2,1)S(1)}, u32[]{:S(2)}, u32[]{:S(2)}) collective-permute-start(bf16[2,32,1500]{2,1,0:T(8,128)(2,1)S(1)} %get-tuple-element.56), channel_id=1, source_target_pairs={{0,1},{1,0},{2,3},{3,2},{4,5},{5,4},{6,7},{7,6},{8,9},{9,8},{10,11... | collective-permute-start | bytes 576008 | tf_op jit(solution)/shard_map/ppermute | solution.py:48
  42.1 39.9 %slice-start.3 = ((s8[9216000]{0:T(1024)(128)(4,1)}), s8[4194304]{0:T(1024)(128)(4,1)S(1)}, s32[]{:S(2)}) async-start(s8[9216000]{0:T(1024)(128)(4,1)} %bitcast.114), calls=%async_computation.3 | async-start | bytes 8388608
  42.2 11.9 %collective-permute-start.11 = (f16[2,64,1500]{2,1,0:T(8,128)(2,1)S(1)}, f16[2,64,1500]{2,1,0:T(8,128)(2,1)S(1)}, u32[]{:S(2)}, u32[]{:S(2)}) collective-permute-start(f16[2,64,1500]{2,1,0:T(8,128)(2,1)S(1)} %get-tuple-element.35), channel_id=1, source_target_pairs={{0,96},{1,33},{2,98},{3,35},{4,100},{5,37},{6,102},{7,39},{8,104},... | collective-permute-start | bytes 1152008 | tf_op jit(solution)/shard_map/ppermute | solution.py:48
  45.5 11.6 %collective-permute-start.4 = (bf16[2,2,32,1500]{3,2,1,0:T(8,128)(2,1)S(1)}, bf16[2,2,32,1500]{3,2,1,0:T(8,128)(2,1)S(1)}, u32[]{:S(2)}, u32[]{:S(2)}) collective-permute-start(bf16[2,2,32,1500]{3,2,1,0:T(8,128)(2,1)S(1)} %copy.6), channel_id=1, source_target_pairs={{0,96},{1,33},{2,98},{3,35},{4,100},{5,37},{6,102},{7,39},{8,104},... | collective-permute-start | bytes 1152008 | tf_op jit(solution)/shard_map/ppermute | solution.py:48
  50.4 31.6 %slice-start.4 = ((s8[9216000]{0:T(1024)(128)(4,1)}), s8[4194304]{0:T(1024)(128)(4,1)S(1)}, s32[]{:S(2)}) async-start(s8[9216000]{0:T(1024)(128)(4,1)} %bitcast.114), calls=%async_computation.4 | async-start | bytes 8388608
  50.8 11.2 %collective-permute-start.17 = (f16[2,64,1500]{2,1,0:T(8,128)(2,1)S(1)}, f16[2,64,1500]{2,1,0:T(8,128)(2,1)S(1)}, u32[]{:S(2)}, u32[]{:S(2)}) collective-permute-start(f16[2,64,1500]{2,1,0:T(8,128)(2,1)S(1)} %get-tuple-element.39), channel_id=1, source_target_pairs={{0,96},{1,33},{2,98},{3,35},{4,100},{5,37},{6,102},{7,39},{8,104},... | collective-permute-start | bytes 1152008 | tf_op jit(solution)/shard_map/ppermute | solution.py:48
  54.2 12.1 %collective-permute-start.13 = (f16[2,64,1500]{2,1,0:T(8,128)(2,1)S(1)}, f16[2,64,1500]{2,1,0:T(8,128)(2,1)S(1)}, u32[]{:S(2)}, u32[]{:S(2)}) collective-permute-start(f16[2,64,1500]{2,1,0:T(8,128)(2,1)S(1)} %get-tuple-element.29), channel_id=1, source_target_pairs={{0,16},{16,0},{32,48},{48,32},{64,80},{80,64},{96,112},{112,96},{1... | collective-permute-start | bytes 1152008 | tf_op jit(solution)/shard_map/ppermute | solution.py:48
  57.1 21.3 %collective-permute-start.5 = (bf16[2,2,2,32,1500]{4,3,2,1,0:T(8,128)(2,1)S(1)}, bf16[2,2,2,32,1500]{4,3,2,1,0:T(8,128)(2,1)S(1)}, u32[]{:S(2)}, u32[]{:S(2)}) collective-permute-start(bf16[2,2,2,32,1500]{4,3,2,1,0:T(8,128)(2,1)S(1)} %pad_maximum_fusion.2.near), channel_id=1, source_target_pairs={{0,32},{1,97},{2,34},{3,99},{4,36},{5,101},{6,38},{7,103},{8,40},{... | collective-permute-start | bytes 2304008 | tf_op jit(solution)/shard_map/ppermute | solution.py:48
  57.2 24.8 %slice-start.5 = ((s8[9216000]{0:T(1024)(128)(4,1)}), s8[827392]{0:T(1024)(128)(4,1)S(1)}, s32[]{:S(2)}) async-start(s8[9216000]{0:T(1024)(128)(4,1)} %bitcast.114), calls=%async_computation.5 | async-start | bytes 1654784
  62.1 11.4 %collective-permute-start.18 = (f16[2,64,1500]{2,1,0:T(8,128)(2,1)S(1)}, f16[2,64,1500]{2,1,0:T(8,128)(2,1)S(1)}, u32[]{:S(2)}, u32[]{:S(2)}) collective-permute-start(f16[2,64,1500]{2,1,0:T(8,128)(2,1)S(1)} %get-tuple-element.33), channel_id=1, source_target_pairs={{0,16},{16,0},{32,48},{48,32},{64,80},{80,64},{96,112},{112,96},{1... | collective-permute-start | bytes 1152008 | tf_op jit(solution)/shard_map/ppermute | solution.py:48
  73.6 1.5 collective-permute-start.19
  73.7 17.1 %collective-permute-start.14 = (bf16[2,32,1500]{2,1,0:T(8,128)(2,1)S(1)}, bf16[2,32,1500]{2,1,0:T(8,128)(2,1)S(1)}, u32[]{:S(2)}, u32[]{:S(2)}) collective-permute-start(bf16[2,32,1500]{2,1,0:T(8,128)(2,1)S(1)} %get-tuple-element.54), channel_id=1, source_target_pairs={{0,1},{1,0},{2,3},{3,2},{4,5},{5,4},{6,7},{7,6},{8,9},{9,8},{10,11... | collective-permute-start | bytes 576008 | tf_op jit(solution)/shard_map/ppermute | solution.py:48
  75.2 15.5 %collective-permute-start.20 = (bf16[2,2,32,1500]{3,2,1,0:T(8,128)(2,1)S(1)}, bf16[2,2,32,1500]{3,2,1,0:T(8,128)(2,1)S(1)}, u32[]{:S(2)}, u32[]{:S(2)}) collective-permute-start(bf16[2,2,32,1500]{3,2,1,0:T(8,128)(2,1)S(1)} %pad_maximum_fusion.11), channel_id=1, source_target_pairs={{0,96},{1,33},{2,98},{3,35},{4,100},{5,37},{6,102},{7,39},{8,104},... | collective-permute-start | bytes 1152008 | tf_op jit(solution)/shard_map/ppermute | solution.py:48
  78.4 3.6 %copy-start.2 = (bf16[1500,3000]{0,1:T(8,128)(2,1)}, bf16[1500,3000]{0,1:T(8,128)(2,1)S(1)}, u32[]{:S(2)}) copy-start(bf16[1500,3000]{0,1:T(8,128)(2,1)S(1)} %collective-permute-done.6) | copy-start | bytes 27000004
  90.8 15.4 %collective-permute-start.21 = (bf16[2,2,2,32,1500]{4,3,2,1,0:T(8,128)(2,1)S(1)}, bf16[2,2,2,32,1500]{4,3,2,1,0:T(8,128)(2,1)S(1)}, u32[]{:S(2)}, u32[]{:S(2)}) collective-permute-start(bf16[2,2,2,32,1500]{4,3,2,1,0:T(8,128)(2,1)S(1)} %pad_maximum_fusion.8.near), channel_id=1, source_target_pairs={{0,32},{1,97},{2,34},{3,99},{4,36},{5,101},{6,38},{7,103},{8,40},{... | collective-permute-start | bytes 2304008 | tf_op jit(solution)/shard_map/ppermute | solution.py:48
  91.0 13.3 %collective-permute-start.15 = (bf16[2,2,32,1500]{3,2,1,0:T(8,128)(2,1)S(1)}, bf16[2,2,32,1500]{3,2,1,0:T(8,128)(2,1)S(1)}, u32[]{:S(2)}, u32[]{:S(2)}) collective-permute-start(bf16[2,2,32,1500]{3,2,1,0:T(8,128)(2,1)S(1)} %copy.11), channel_id=1, source_target_pairs={{0,96},{1,33},{2,98},{3,35},{4,100},{5,37},{6,102},{7,39},{8,104},... | collective-permute-start | bytes 1152008 | tf_op jit(solution)/shard_map/ppermute | solution.py:48
  91.1 25.6 %collective-permute-start.7 = (bf16[1,2,64,3000]{3,2,1,0:T(8,128)(2,1)S(1)}, bf16[1,2,64,3000]{3,2,1,0:T(8,128)(2,1)S(1)}, u32[]{:S(2)}, u32[]{:S(2)}) collective-permute-start(bf16[1,2,64,3000]{3,2,1,0:T(8,128)(2,1)S(1)} %get-tuple-element.18), channel_id=1, source_target_pairs={{0,2},{1,7},{2,0},{3,5},{4,6},{5,3},{6,4},{7,1},{8,10},{9,15},{10,... | collective-permute-start | bytes 2304008 | tf_op jit(solution)/shard_map/ppermute | solution.py:48
  104.4 15.3 %collective-permute-start.16 = (bf16[2,2,2,32,1500]{4,3,2,1,0:T(8,128)(2,1)S(1)}, bf16[2,2,2,32,1500]{4,3,2,1,0:T(8,128)(2,1)S(1)}, u32[]{:S(2)}, u32[]{:S(2)}) collective-permute-start(bf16[2,2,2,32,1500]{4,3,2,1,0:T(8,128)(2,1)S(1)} %pad_maximum_fusion.7.near), channel_id=1, source_target_pairs={{0,32},{1,97},{2,34},{3,99},{4,36},{5,101},{6,38},{7,103},{8,40},{... | collective-permute-start | bytes 2304008 | tf_op jit(solution)/shard_map/ppermute | solution.py:48
  114.8 16.4 %collective-permute-start.22 = (bf16[1,2,64,3000]{3,2,1,0:T(8,128)(2,1)S(1)}, bf16[1,2,64,3000]{3,2,1,0:T(8,128)(2,1)S(1)}, u32[]{:S(2)}, u32[]{:S(2)}) collective-permute-start(bf16[1,2,64,3000]{3,2,1,0:T(8,128)(2,1)S(1)} %get-tuple-element.26), channel_id=1, source_target_pairs={{0,2},{1,7},{2,0},{3,5},{4,6},{5,3},{6,4},{7,1},{8,10},{9,15},{10,... | collective-permute-start | bytes 2304008 | tf_op jit(solution)/shard_map/ppermute | solution.py:48
  117.0 13.3 %collective-permute-start.8 = (bf16[1,64,3000]{2,1,0:T(8,128)(2,1)S(1)}, bf16[1,64,3000]{2,1,0:T(8,128)(2,1)S(1)}, u32[]{:S(2)}, u32[]{:S(2)}) collective-permute-start(bf16[1,64,3000]{2,1,0:T(8,128)(2,1)S(1)} %fusion.80), channel_id=1, source_target_pairs={{0,6},{1,3},{2,4},{3,1},{4,2},{5,7},{6,0},{7,5},{8,14},{9,11},{10,... | collective-permute-start | bytes 1152008 | tf_op jit(solution)/shard_map/ppermute | solution.py:48
  128.3 16.3 %collective-permute-start.23 = (bf16[1,2,64,3000]{3,2,1,0:T(8,128)(2,1)S(1)}, bf16[1,2,64,3000]{3,2,1,0:T(8,128)(2,1)S(1)}, u32[]{:S(2)}, u32[]{:S(2)}) collective-permute-start(bf16[1,2,64,3000]{3,2,1,0:T(8,128)(2,1)S(1)} %get-tuple-element.28), channel_id=1, source_target_pairs={{0,2},{1,7},{2,0},{3,5},{4,6},{5,3},{6,4},{7,1},{8,10},{9,15},{10,... | collective-permute-start | bytes 2304008 | tf_op jit(solution)/shard_map/ppermute | solution.py:48
  130.5 30.0 %collective-permute-start.9 = (bf16[32,3000]{1,0:T(8,128)(2,1)S(1)}, bf16[32,3000]{1,0:T(8,128)(2,1)S(1)}, u32[]{:S(2)}, u32[]{:S(2)}) collective-permute-start(bf16[32,3000]{1,0:T(8,128)(2,1)S(1)} %fusion.107), channel_id=1, source_target_pairs={{0,8},{1,9},{2,10},{3,11},{4,12},{5,13},{6,14},{7,15},{8,0},{9,1},... | collective-permute-start | bytes 576008 | tf_op jit(solution)/shard_map/ppermute | solution.py:48
  131.4 14.4 %collective-permute-start.26 = (bf16[1,64,3000]{2,1,0:T(8,128)(2,1)S(1)}, bf16[1,64,3000]{2,1,0:T(8,128)(2,1)S(1)}, u32[]{:S(2)}, u32[]{:S(2)}) collective-permute-start(bf16[1,64,3000]{2,1,0:T(8,128)(2,1)S(1)} %fusion.84), channel_id=1, source_target_pairs={{0,6},{1,3},{2,4},{3,1},{4,2},{5,7},{6,0},{7,5},{8,14},{9,11},{10,... | collective-permute-start | bytes 1152008 | tf_op jit(solution)/shard_map/ppermute | solution.py:48
  144.9 9.1 %collective-permute-start.24 = (bf16[1,64,3000]{2,1,0:T(8,128)(2,1)S(1)}, bf16[1,64,3000]{2,1,0:T(8,128)(2,1)S(1)}, u32[]{:S(2)}, u32[]{:S(2)}) collective-permute-start(bf16[1,64,3000]{2,1,0:T(8,128)(2,1)S(1)} %fusion.83), channel_id=1, source_target_pairs={{0,6},{1,3},{2,4},{3,1},{4,2},{5,7},{6,0},{7,5},{8,14},{9,11},{10,... | collective-permute-start | bytes 1152008 | tf_op jit(solution)/shard_map/ppermute | solution.py:48
  145.9 8.8 %collective-permute-start.27 = (bf16[32,3000]{1,0:T(8,128)(2,1)S(1)}, bf16[32,3000]{1,0:T(8,128)(2,1)S(1)}, u32[]{:S(2)}, u32[]{:S(2)}) collective-permute-start(bf16[32,3000]{1,0:T(8,128)(2,1)S(1)} %fusion.109), channel_id=1, source_target_pairs={{0,8},{1,9},{2,10},{3,11},{4,12},{5,13},{6,14},{7,15},{8,0},{9,1},... | collective-permute-start | bytes 576008 | tf_op jit(solution)/shard_map/ppermute | solution.py:48
  154.1 5.7 %collective-permute-start.25 = (bf16[32,3000]{1,0:T(8,128)(2,1)S(1)}, bf16[32,3000]{1,0:T(8,128)(2,1)S(1)}, u32[]{:S(2)}, u32[]{:S(2)}) collective-permute-start(bf16[32,3000]{1,0:T(8,128)(2,1)S(1)} %fusion.108), channel_id=1, source_target_pairs={{0,8},{1,9},{2,10},{3,11},{4,12},{5,13},{6,14},{7,15},{8,0},{9,1},... | collective-permute-start | bytes 576008 | tf_op jit(solution)/shard_map/ppermute | solution.py:48
  159.9 2.3 %copy-start.1 = (bf16[1000,768]{1,0:T(8,128)(2,1)S(1)}, bf16[1000,768]{1,0:T(8,128)(2,1)}, u32[]{:S(2)}) copy-start(bf16[1000,768]{1,0:T(8,128)(2,1)} %param.4) | copy-start | bytes 4608004

commit v4 on v3

--- a/solution.py
+++ b/solution.py
@@ -9,7 +9,7 @@
 NY, NH, NL, NZ, NC = 4, 2, 2, 4, 2
 PARTS = (4, 4, 4)
 SCALE = 16.0
-TILE = 512
+TILE = 768
 
 SWAP_H = [(i, i ^ 1) for i in range(NY * NH)]
 SWAP_CORE = [(i, i ^ 1) for i in range(NL * NZ * NC)]

time: 163 us -> 160 us (0.982)
  Pallas kernels: 25.9 us -> 23.6 us
    pallas_call x3, Pallas kernels: 25.9 us -> 23.6 us  [fit(): pl.pallas_call(fit_kernel, grid=(pl.cdiv(n_cols, TILE),), in_specs=[units...]
  transfers between devices with their start and end apart: 28 -> 28, of which waited for: 14 -> 14; matrix products, arithmetic and copies ran while one was open for 7% -> 7% of each run, Pallas kernels for 16% -> 15%
where the time goes in v4:
time: 160 us
  waiting for transfers between devices  69.5 us (43%)
  starting transfers between devices  43.4 us (27%)
  Pallas kernels  23.6 us (15%)
  matrix products  11 us (7%)
  local copies, waits for them, and re-layouts  8.39 us (5%)
  other arithmetic  3.45 us (2%)
    ppermute x27, waiting for transfers between devices, permuted(): return by_rows(lax.ppermute(by_rows(x), axis, pairs))  69.5 us
    ppermute x27, starting transfers between devices, permuted(): return by_rows(lax.ppermute(by_rows(x), axis, pairs))  42.4 us
    pallas_call x3, Pallas kernels, fit(): pl.pallas_call(fit_kernel, grid=(pl.cdiv(n_cols, TILE),), in_specs=[units...  23.6 us
    unnamed x20, local copies, waits for them, and re-layouts  7.02 us
    dot_general x6, matrix products, partial_sums(): lax.dot_general(cols, half, (((0,), (0,)), ((), ())), preferred_element_t...  6.04 us
  transfers between devices with their start and end apart: 28, of which 14 were waited for; matrix products, arithmetic and copies ran while one was open for 7% of the time, Pallas kernels for 15%

profile of v4, /device:TPU:0, one launch (start us, length us, event | category | flops | bytes accessed | tf_op | source)
XLA Modules:
  0.0 159.9 jit_solution(380719099795913391)
XLA Ops:
  0.1 1.3 copy-done
  2.1 2.1 %copy-done.3 = bf16[2,1000,1500]{2,1,0:T(8,128)(2,1)S(1)} copy-done((bf16[2,1000,1500]{2,1,0:T(8,128)(2,1)S(1)}, bf16[2,1000,1500]{2,1,0:T(8,128)(2,1)}, u32[]{:S(2)}) %copy-start.3) | copy-done | bytes 6000024
  4.1 1.0 fusion.37
  5.2 1.0 fusion.46
  6.7 1.8 %collective-permute-start = (f16[2,2,64,1500]{3,2,1,0:T(8,128)(2,1)S(1)}, f16[2,2,64,1500]{3,2,1,0:T(8,128)(2,1)S(1)}, u32[]{:S(2)}, u32[]{:S(2)}) collective-permute-start(f16[2,2,64,1500]{3,2,1,0:T(8,128)(2,1)S(1)} %pad_maximum_fusion.1), channel_id=1, source_target_pairs={{0,32},{1,97},{2,34},{3,99},{4,36},{5,101},{6,38},{7,103},{8,40},{... | collective-permute-start | bytes 2304008 | tf_op jit(solution)/shard_map/ppermute | solution.py:48
  8.4 1.1 collective-permute-start.6
  9.5 0.7 convolution_convert_fusion
  10.1 0.7 convolution_convert_fusion.1
  10.8 1.0 fusion.34
  11.8 1.0 fusion.43
  13.1 1.0 fusion.31
  14.3 1.0 fusion.40
  15.4 3.3 %collective-permute-done = f16[2,2,64,1500]{3,2,1,0:T(8,128)(2,1)S(1)} collective-permute-done((f16[2,2,64,1500]{3,2,1,0:T(8,128)(2,1)S(1)}, f16[2,2,64,1500]{3,2,1,0:T(8,128)(2,1)S(1)}, u32[]{:S(2)}, u32[]{:S(2)}) %collective-permute-start) | collective-permute-done | bytes 768032 | tf_op jit(solution)/shard_map/ppermute | solution.py:48
  19.1 3.2 %collective-permute-start.1 = (f16[2,64,1500]{2,1,0:T(8,128)(2,1)S(1)}, f16[2,64,1500]{2,1,0:T(8,128)(2,1)S(1)}, u32[]{:S(2)}, u32[]{:S(2)}) collective-permute-start(f16[2,64,1500]{2,1,0:T(8,128)(2,1)S(1)} %get-tuple-element.37), channel_id=1, source_target_pairs={{0,96},{1,33},{2,98},{3,35},{4,100},{5,37},{6,102},{7,39},{8,104},... | collective-permute-start | bytes 1152008 | tf_op jit(solution)/shard_map/ppermute | solution.py:48
  22.9 9.5 %collective-permute-done.1 = f16[2,64,1500]{2,1,0:T(8,128)(2,1)S(1)} collective-permute-done((f16[2,64,1500]{2,1,0:T(8,128)(2,1)S(1)}, f16[2,64,1500]{2,1,0:T(8,128)(2,1)S(1)}, u32[]{:S(2)}, u32[]{:S(2)}) %collective-permute-start.1) | collective-permute-done | bytes 384032 | tf_op jit(solution)/shard_map/ppermute | solution.py:48
  32.5 3.1 %collective-permute-start.2 = (f16[2,64,1500]{2,1,0:T(8,128)(2,1)S(1)}, f16[2,64,1500]{2,1,0:T(8,128)(2,1)S(1)}, u32[]{:S(2)}, u32[]{:S(2)}) collective-permute-start(f16[2,64,1500]{2,1,0:T(8,128)(2,1)S(1)} %get-tuple-element.31), channel_id=1, source_target_pairs={{0,16},{16,0},{32,48},{48,32},{64,80},{80,64},{96,112},{112,96},{1... | collective-permute-start | bytes 1152008 | tf_op jit(solution)/shard_map/ppermute | solution.py:48
  36.4 5.5 %collective-permute-done.2 = f16[2,64,1500]{2,1,0:T(8,128)(2,1)S(1)} collective-permute-done((f16[2,64,1500]{2,1,0:T(8,128)(2,1)S(1)}, f16[2,64,1500]{2,1,0:T(8,128)(2,1)S(1)}, u32[]{:S(2)}, u32[]{:S(2)}) %collective-permute-start.2) | collective-permute-done | bytes 384032 | tf_op jit(solution)/shard_map/ppermute | solution.py:48
  42.2 3.1 %collective-permute-start.11 = (f16[2,64,1500]{2,1,0:T(8,128)(2,1)S(1)}, f16[2,64,1500]{2,1,0:T(8,128)(2,1)S(1)}, u32[]{:S(2)}, u32[]{:S(2)}) collective-permute-start(f16[2,64,1500]{2,1,0:T(8,128)(2,1)S(1)} %get-tuple-element.35), channel_id=1, source_target_pairs={{0,96},{1,33},{2,98},{3,35},{4,100},{5,37},{6,102},{7,39},{8,104},... | collective-permute-start | bytes 1152008 | tf_op jit(solution)/shard_map/ppermute | solution.py:48
  45.5 1.3 collective-permute-start.4
  46.8 3.6 %collective-permute-done.12 = f16[2,2,64,1500]{3,2,1,0:T(8,128)(2,1)S(1)} collective-permute-done((f16[2,2,64,1500]{3,2,1,0:T(8,128)(2,1)S(1)}, f16[2,2,64,1500]{3,2,1,0:T(8,128)(2,1)S(1)}, u32[]{:S(2)}, u32[]{:S(2)}) %collective-permute-start.12) | collective-permute-done | bytes 768032 | tf_op jit(solution)/shard_map/ppermute | solution.py:48
  50.8 3.3 %collective-permute-start.17 = (f16[2,64,1500]{2,1,0:T(8,128)(2,1)S(1)}, f16[2,64,1500]{2,1,0:T(8,128)(2,1)S(1)}, u32[]{:S(2)}, u32[]{:S(2)}) collective-permute-start(f16[2,64,1500]{2,1,0:T(8,128)(2,1)S(1)} %get-tuple-element.39), channel_id=1, source_target_pairs={{0,96},{1,33},{2,98},{3,35},{4,100},{5,37},{6,102},{7,39},{8,104},... | collective-permute-start | bytes 1152008 | tf_op jit(solution)/shard_map/ppermute | solution.py:48
  54.2 1.9 %collective-permute-start.13 = (f16[2,64,1500]{2,1,0:T(8,128)(2,1)S(1)}, f16[2,64,1500]{2,1,0:T(8,128)(2,1)S(1)}, u32[]{:S(2)}, u32[]{:S(2)}) collective-permute-start(f16[2,64,1500]{2,1,0:T(8,128)(2,1)S(1)} %get-tuple-element.29), channel_id=1, source_target_pairs={{0,16},{16,0},{32,48},{48,32},{64,80},{80,64},{96,112},{112,96},{1... | collective-permute-start | bytes 1152008 | tf_op jit(solution)/shard_map/ppermute | solution.py:48
  56.1 1.0 collective-permute-done.4
  57.3 4.7 %collective-permute-done.17 = f16[2,64,1500]{2,1,0:T(8,128)(2,1)S(1)} collective-permute-done((f16[2,64,1500]{2,1,0:T(8,128)(2,1)S(1)}, f16[2,64,1500]{2,1,0:T(8,128)(2,1)S(1)}, u32[]{:S(2)}, u32[]{:S(2)}) %collective-permute-start.17) | collective-permute-done | bytes 384032 | tf_op jit(solution)/shard_map/ppermute | solution.py:48
  62.1 4.3 %collective-permute-start.18 = (f16[2,64,1500]{2,1,0:T(8,128)(2,1)S(1)}, f16[2,64,1500]{2,1,0:T(8,128)(2,1)S(1)}, u32[]{:S(2)}, u32[]{:S(2)}) collective-permute-start(f16[2,64,1500]{2,1,0:T(8,128)(2,1)S(1)} %get-tuple-element.33), channel_id=1, source_target_pairs={{0,16},{16,0},{32,48},{48,32},{64,80},{80,64},{96,112},{112,96},{1... | collective-permute-start | bytes 1152008 | tf_op jit(solution)/shard_map/ppermute | solution.py:48
  66.5 7.0 %collective-permute-done.18 = f16[2,64,1500]{2,1,0:T(8,128)(2,1)S(1)} collective-permute-done((f16[2,64,1500]{2,1,0:T(8,128)(2,1)S(1)}, f16[2,64,1500]{2,1,0:T(8,128)(2,1)S(1)}, u32[]{:S(2)}, u32[]{:S(2)}) %collective-permute-start.18) | collective-permute-done | bytes 384032 | tf_op jit(solution)/shard_map/ppermute | solution.py:48
  74.3 0.8 collective-permute-done.19
  75.2 3.3 %collective-permute-start.20 = (bf16[2,2,32,1500]{3,2,1,0:T(8,128)(2,1)S(1)}, bf16[2,2,32,1500]{3,2,1,0:T(8,128)(2,1)S(1)}, u32[]{:S(2)}, u32[]{:S(2)}) collective-permute-start(bf16[2,2,32,1500]{3,2,1,0:T(8,128)(2,1)S(1)} %pad_maximum_fusion.11), channel_id=1, source_target_pairs={{0,96},{1,33},{2,98},{3,35},{4,100},{5,37},{6,102},{7,39},{8,104},... | collective-permute-start | bytes 1152008 | tf_op jit(solution)/shard_map/ppermute | solution.py:48
  78.4 3.6 %copy-done.2 = bf16[1500,3000]{0,1:T(8,128)(2,1)} copy-done((bf16[1500,3000]{0,1:T(8,128)(2,1)}, bf16[1500,3000]{0,1:T(8,128)(2,1)S(1)}, u32[]{:S(2)}) %copy-start.2) | copy-done | bytes 9000024
  82.0 7.9 %shard_map.37 = (bf16[1,2,64,3000]{3,2,1,0:T(8,128)(2,1)S(1)}, f32[1,2,64,3000]{3,2,1,0:T(8,128)S(1)}) custom-call(bf16[2,2,2,32,1500]{4,3,2,1,0:T(8,128)(2,1)S(1)} %pad_maximum_fusion.2.near, bf16[2,2,2,32,1500]{4,3,2,1,0:T(8,128)(2,1)S(1)} %collective-permute-done.5.far, bf16[3000,1500]{1,0:T(8,128)(2,1)S(1)} %bitcast.116, bf16[3000,1500]{1,0:T(8,128)(2,1)} %bitcast.119), custom_call_target="tpu_custom_call" | custom-call | flops 4608000000 | bytes 20304000 | tf_op jit(solution)/shard_map/pallas_call | solution.py:131
  90.3 2.0 %collective-permute-start.7 = (bf16[1,2,64,3000]{3,2,1,0:T(8,128)(2,1)S(1)}, bf16[1,2,64,3000]{3,2,1,0:T(8,128)(2,1)S(1)}, u32[]{:S(2)}, u32[]{:S(2)}) collective-permute-start(bf16[1,2,64,3000]{3,2,1,0:T(8,128)(2,1)S(1)} %get-tuple-element.18), channel_id=1, source_target_pairs={{0,2},{1,7},{2,0},{3,5},{4,6},{5,3},{6,4},{7,1},{8,10},{9,15},{10,... | collective-permute-start | bytes 2304008 | tf_op jit(solution)/shard_map/ppermute | solution.py:48
  92.3 11.2 %collective-permute-done.15 = bf16[2,2,32,1500]{3,2,1,0:T(8,128)(2,1)S(1)} collective-permute-done((bf16[2,2,32,1500]{3,2,1,0:T(8,128)(2,1)S(1)}, bf16[2,2,32,1500]{3,2,1,0:T(8,128)(2,1)S(1)}, u32[]{:S(2)}, u32[]{:S(2)}) %collective-permute-start.15) | collective-permute-done | bytes 384032 | tf_op jit(solution)/shard_map/ppermute | solution.py:48
  103.6 0.9 collective-permute-start.16
  104.5 0.9 collective-permute-done.21.far
  105.4 7.9 %shard_map.39 = (bf16[1,2,64,3000]{3,2,1,0:T(8,128)(2,1)S(1)}, f32[1,2,64,3000]{3,2,1,0:T(8,128)S(1)}) custom-call(bf16[2,2,2,32,1500]{4,3,2,1,0:T(8,128)(2,1)S(1)} %pad_maximum_fusion.8.near, bf16[2,2,2,32,1500]{4,3,2,1,0:T(8,128)(2,1)S(1)} %collective-permute-done.21.far, bf16[3000,1500]{1,0:T(8,128)(2,1)S(1)} %bitcast.117, bf16[3000,1500]{1,0:T(8,128)(2,1)} %bitcast.120), custom_call_target="tpu_custom_call" | custom-call | flops 4608000000 | bytes 20304000 | tf_op jit(solution)/shard_map/pallas_call | solution.py:131
  113.2 2.0 %collective-permute-start.22 = (bf16[1,2,64,3000]{3,2,1,0:T(8,128)(2,1)S(1)}, bf16[1,2,64,3000]{3,2,1,0:T(8,128)(2,1)S(1)}, u32[]{:S(2)}, u32[]{:S(2)}) collective-permute-start(bf16[1,2,64,3000]{3,2,1,0:T(8,128)(2,1)S(1)} %get-tuple-element.26), channel_id=1, source_target_pairs={{0,2},{1,7},{2,0},{3,5},{4,6},{5,3},{6,4},{7,1},{8,10},{9,15},{10,... | collective-permute-start | bytes 2304008 | tf_op jit(solution)/shard_map/ppermute | solution.py:48
  115.5 2.6 %collective-permute-start.8 = (bf16[1,64,3000]{2,1,0:T(8,128)(2,1)S(1)}, bf16[1,64,3000]{2,1,0:T(8,128)(2,1)S(1)}, u32[]{:S(2)}, u32[]{:S(2)}) collective-permute-start(bf16[1,64,3000]{2,1,0:T(8,128)(2,1)S(1)} %fusion.80), channel_id=1, source_target_pairs={{0,6},{1,3},{2,4},{3,1},{4,2},{5,7},{6,0},{7,5},{8,14},{9,11},{10,... | collective-permute-start | bytes 1152008 | tf_op jit(solution)/shard_map/ppermute | solution.py:48
  118.1 7.9 %shard_map.38 = (bf16[1,2,64,3000]{3,2,1,0:T(8,128)(2,1)S(1)}, f32[1,2,64,3000]{3,2,1,0:T(8,128)S(1)}) custom-call(bf16[2,2,2,32,1500]{4,3,2,1,0:T(8,128)(2,1)S(1)} %pad_maximum_fusion.7.near, bf16[2,2,2,32,1500]{4,3,2,1,0:T(8,128)(2,1)S(1)} %collective-permute-done.16.far, bf16[3000,1500]{1,0:T(8,128)(2,1)S(1)} %bitcast.118, bf16[3000,1500]{1,0:T(8,128)(2,1)} %bitcast.121), custom_call_target="tpu_custom_call" | custom-call | flops 4608000000 | bytes 20304000 | tf_op jit(solution)/shard_map/pallas_call | solution.py:131
  126.0 1.1 collective-permute-start.23
  127.1 1.8 %collective-permute-done.8 = bf16[1,64,3000]{2,1,0:T(8,128)(2,1)S(1)} collective-permute-done((bf16[1,64,3000]{2,1,0:T(8,128)(2,1)S(1)}, bf16[1,64,3000]{2,1,0:T(8,128)(2,1)S(1)}, u32[]{:S(2)}, u32[]{:S(2)}) %collective-permute-start.8) | collective-permute-done | bytes 384032 | tf_op jit(solution)/shard_map/ppermute | solution.py:48
  129.0 0.7 collective-permute-start.9
  129.9 2.6 %collective-permute-start.26 = (bf16[1,64,3000]{2,1,0:T(8,128)(2,1)S(1)}, bf16[1,64,3000]{2,1,0:T(8,128)(2,1)S(1)}, u32[]{:S(2)}, u32[]{:S(2)}) collective-permute-start(bf16[1,64,3000]{2,1,0:T(8,128)(2,1)S(1)} %fusion.84), channel_id=1, source_target_pairs={{0,6},{1,3},{2,4},{3,1},{4,2},{5,7},{6,0},{7,5},{8,14},{9,11},{10,... | collective-permute-start | bytes 1152008 | tf_op jit(solution)/shard_map/ppermute | solution.py:48
  132.5 9.7 %collective-permute-done.23 = bf16[1,2,64,3000]{3,2,1,0:T(8,128)(2,1)S(1)} collective-permute-done((bf16[1,2,64,3000]{3,2,1,0:T(8,128)(2,1)S(1)}, bf16[1,2,64,3000]{3,2,1,0:T(8,128)(2,1)S(1)}, u32[]{:S(2)}, u32[]{:S(2)}) %collective-permute-start.23) | collective-permute-done | bytes 768032 | tf_op jit(solution)/shard_map/ppermute | solution.py:48
  142.6 1.7 %collective-permute-start.24 = (bf16[1,64,3000]{2,1,0:T(8,128)(2,1)S(1)}, bf16[1,64,3000]{2,1,0:T(8,128)(2,1)S(1)}, u32[]{:S(2)}, u32[]{:S(2)}) collective-permute-start(bf16[1,64,3000]{2,1,0:T(8,128)(2,1)S(1)} %fusion.83), channel_id=1, source_target_pairs={{0,6},{1,3},{2,4},{3,1},{4,2},{5,7},{6,0},{7,5},{8,14},{9,11},{10,... | collective-permute-start | bytes 1152008 | tf_op jit(solution)/shard_map/ppermute | solution.py:48
  144.4 1.3 collective-permute-start.27
  145.7 6.0 %collective-permute-done.24 = bf16[1,64,3000]{2,1,0:T(8,128)(2,1)S(1)} collective-permute-done((bf16[1,64,3000]{2,1,0:T(8,128)(2,1)S(1)}, bf16[1,64,3000]{2,1,0:T(8,128)(2,1)S(1)}, u32[]{:S(2)}, u32[]{:S(2)}) %collective-permute-start.24) | collective-permute-done | bytes 384032 | tf_op jit(solution)/shard_map/ppermute | solution.py:48
  153.1 4.5 %collective-permute-done.25 = bf16[32,3000]{1,0:T(8,128)(2,1)S(1)} collective-permute-done((bf16[32,3000]{1,0:T(8,128)(2,1)S(1)}, bf16[32,3000]{1,0:T(8,128)(2,1)S(1)}, u32[]{:S(2)}, u32[]{:S(2)}) %collective-permute-start.25) | collective-permute-done | bytes 192032 | tf_op jit(solution)/shard_map/ppermute | solution.py:48
  158.2 1.7 %fusion = f32[96,3000]{1,0:T(8,128)} fusion(f32[96,3000]{1,0:T(8,128)S(1)} %fusion.85, f32[96,3000]{1,0:T(8,128)S(1)} %fusion.88, f32[32,3000]{1,0:T(8,128)S(1)} %slice_bitcast_fusion.8, bf16[32,3000]{1,0:T(8,128)(2,1)S(1)} %collective-permute-done.9, s32[32]{0:T(128)S(1)} %get-tuple-element.68, s32[32]{0:T(128)S(1)} %get-tuple-element.69, ...), kind=kOutput, calls=%fused_computation.1 | convolution fusion | flops 111464448 | bytes 4032588 | tf_op jit(solution)/shard_map/dot_general | solution.py:84
  (101 shorter events, 9.2 us)
Async XLA Ops:
  0.0 1.4 copy-start
  1.4 2.7 %copy-start.3 = (bf16[2,1000,1500]{2,1,0:T(8,128)(2,1)S(1)}, bf16[2,1000,1500]{2,1,0:T(8,128)(2,1)}, u32[]{:S(2)}) copy-start(bf16[2,1000,1500]{2,1,0:T(8,128)(2,1)} %param.3) | copy-start | bytes 18000004
  4.1 4.3 %slice-start = ((s8[9216000]{0:T(1024)(128)(4,1)}), s8[4194304]{0:T(1024)(128)(4,1)S(1)}, s32[]{:S(2)}) async-start(s8[9216000]{0:T(1024)(128)(4,1)} %bitcast.112), calls=%async_computation | async-start | bytes 8388608
  4.1 4.3 %slice-start.1 = ((s8[9216000]{0:T(1024)(128)(4,1)}), s8[4194304]{0:T(1024)(128)(4,1)S(1)}, s32[]{:S(2)}) async-start(s8[9216000]{0:T(1024)(128)(4,1)} %bitcast.112), calls=%async_computation.1 | async-start | bytes 8388608
  5.2 3.3 %slice-start.2 = ((s8[9216000]{0:T(1024)(128)(4,1)}), s8[827392]{0:T(1024)(128)(4,1)S(1)}, s32[]{:S(2)}) async-start(s8[9216000]{0:T(1024)(128)(4,1)} %bitcast.112), calls=%async_computation.2 | async-start | bytes 1654784
  6.7 12.1 %collective-permute-start = (f16[2,2,64,1500]{3,2,1,0:T(8,128)(2,1)S(1)}, f16[2,2,64,1500]{3,2,1,0:T(8,128)(2,1)S(1)}, u32[]{:S(2)}, u32[]{:S(2)}) collective-permute-start(f16[2,2,64,1500]{3,2,1,0:T(8,128)(2,1)S(1)} %pad_maximum_fusion.1), channel_id=1, source_target_pairs={{0,32},{1,97},{2,34},{3,99},{4,36},{5,101},{6,38},{7,103},{8,40},{... | collective-permute-start | bytes 2304008 | tf_op jit(solution)/shard_map/ppermute | solution.py:48
  8.4 70.0 %collective-permute-start.6 = (bf16[1500,3000]{0,1:T(8,128)(2,1)S(1)}, bf16[1500,3000]{0,1:T(8,128)(2,1)S(1)}, u32[]{:S(2)}, u32[]{:S(2)}) collective-permute-start(bf16[1500,3000]{0,1:T(8,128)(2,1)S(1)} %bitcast.113), channel_id=1, source_target_pairs={{0,1},{1,0},{2,3},{3,2},{4,5},{5,4},{6,7},{7,6},{8,9},{9,8},{10,11... | collective-permute-start | bytes 27000008 | tf_op jit(solution)/shard_map/ppermute | solution.py:98
  19.1 13.3 %collective-permute-start.1 = (f16[2,64,1500]{2,1,0:T(8,128)(2,1)S(1)}, f16[2,64,1500]{2,1,0:T(8,128)(2,1)S(1)}, u32[]{:S(2)}, u32[]{:S(2)}) collective-permute-start(f16[2,64,1500]{2,1,0:T(8,128)(2,1)S(1)} %get-tuple-element.37), channel_id=1, source_target_pairs={{0,96},{1,33},{2,98},{3,35},{4,100},{5,37},{6,102},{7,39},{8,104},... | collective-permute-start | bytes 1152008 | tf_op jit(solution)/shard_map/ppermute | solution.py:48
  22.5 13.1 %collective-permute-start.10 = (f16[2,2,64,1500]{3,2,1,0:T(8,128)(2,1)S(1)}, f16[2,2,64,1500]{3,2,1,0:T(8,128)(2,1)S(1)}, u32[]{:S(2)}, u32[]{:S(2)}) collective-permute-start(f16[2,2,64,1500]{3,2,1,0:T(8,128)(2,1)S(1)} %pad_maximum_fusion.4), channel_id=1, source_target_pairs={{0,32},{1,97},{2,34},{3,99},{4,36},{5,101},{6,38},{7,103},{8,40},{... | collective-permute-start | bytes 2304008 | tf_op jit(solution)/shard_map/ppermute | solution.py:48
  32.5 9.4 %collective-permute-start.2 = (f16[2,64,1500]{2,1,0:T(8,128)(2,1)S(1)}, f16[2,64,1500]{2,1,0:T(8,128)(2,1)S(1)}, u32[]{:S(2)}, u32[]{:S(2)}) collective-permute-start(f16[2,64,1500]{2,1,0:T(8,128)(2,1)S(1)} %get-tuple-element.31), channel_id=1, source_target_pairs={{0,16},{16,0},{32,48},{48,32},{64,80},{80,64},{96,112},{112,96},{1... | collective-permute-start | bytes 1152008 | tf_op jit(solution)/shard_map/ppermute | solution.py:48
  35.9 14.5 %collective-permute-start.12 = (f16[2,2,64,1500]{3,2,1,0:T(8,128)(2,1)S(1)}, f16[2,2,64,1500]{3,2,1,0:T(8,128)(2,1)S(1)}, u32[]{:S(2)}, u32[]{:S(2)}) collective-permute-start(f16[2,2,64,1500]{3,2,1,0:T(8,128)(2,1)S(1)} %pad_maximum_fusion.6), channel_id=1, source_target_pairs={{0,32},{1,97},{2,34},{3,99},{4,36},{5,101},{6,38},{7,103},{8,40},{... | collective-permute-start | bytes 2304008 | tf_op jit(solution)/shard_map/ppermute | solution.py:48
  42.0 3.4 %collective-permute-start.3 = (bf16[2,32,1500]{2,1,0:T(8,128)(2,1)S(1)}, bf16[2,32,1500]{2,1,0:T(8,128)(2,1)S(1)}, u32[]{:S(2)}, u32[]{:S(2)}) collective-permute-start(bf16[2,32,1500]{2,1,0:T(8,128)(2,1)S(1)} %get-tuple-element.56), channel_id=1, source_target_pairs={{0,1},{1,0},{2,3},{3,2},{4,5},{5,4},{6,7},{7,6},{8,9},{9,8},{10,11... | collective-permute-start | bytes 576008 | tf_op jit(solution)/shard_map/ppermute | solution.py:48
  42.1 39.9 %slice-start.3 = ((s8[9216000]{0:T(1024)(128)(4,1)}), s8[4194304]{0:T(1024)(128)(4,1)S(1)}, s32[]{:S(2)}) async-start(s8[9216000]{0:T(1024)(128)(4,1)} %bitcast.114), calls=%async_computation.3 | async-start | bytes 8388608
  42.2 11.9 %collective-permute-start.11 = (f16[2,64,1500]{2,1,0:T(8,128)(2,1)S(1)}, f16[2,64,1500]{2,1,0:T(8,128)(2,1)S(1)}, u32[]{:S(2)}, u32[]{:S(2)}) collective-permute-start(f16[2,64,1500]{2,1,0:T(8,128)(2,1)S(1)} %get-tuple-element.35), channel_id=1, source_target_pairs={{0,96},{1,33},{2,98},{3,35},{4,100},{5,37},{6,102},{7,39},{8,104},... | collective-permute-start | bytes 1152008 | tf_op jit(solution)/shard_map/ppermute | solution.py:48
  45.5 11.6 %collective-permute-start.4 = (bf16[2,2,32,1500]{3,2,1,0:T(8,128)(2,1)S(1)}, bf16[2,2,32,1500]{3,2,1,0:T(8,128)(2,1)S(1)}, u32[]{:S(2)}, u32[]{:S(2)}) collective-permute-start(bf16[2,2,32,1500]{3,2,1,0:T(8,128)(2,1)S(1)} %copy.6), channel_id=1, source_target_pairs={{0,96},{1,33},{2,98},{3,35},{4,100},{5,37},{6,102},{7,39},{8,104},... | collective-permute-start | bytes 1152008 | tf_op jit(solution)/shard_map/ppermute | solution.py:48
  50.4 31.6 %slice-start.4 = ((s8[9216000]{0:T(1024)(128)(4,1)}), s8[4194304]{0:T(1024)(128)(4,1)S(1)}, s32[]{:S(2)}) async-start(s8[9216000]{0:T(1024)(128)(4,1)} %bitcast.114), calls=%async_computation.4 | async-start | bytes 8388608
  50.8 11.2 %collective-permute-start.17 = (f16[2,64,1500]{2,1,0:T(8,128)(2,1)S(1)}, f16[2,64,1500]{2,1,0:T(8,128)(2,1)S(1)}, u32[]{:S(2)}, u32[]{:S(2)}) collective-permute-start(f16[2,64,1500]{2,1,0:T(8,128)(2,1)S(1)} %get-tuple-element.39), channel_id=1, source_target_pairs={{0,96},{1,33},{2,98},{3,35},{4,100},{5,37},{6,102},{7,39},{8,104},... | collective-permute-start | bytes 1152008 | tf_op jit(solution)/shard_map/ppermute | solution.py:48
  54.2 12.1 %collective-permute-start.13 = (f16[2,64,1500]{2,1,0:T(8,128)(2,1)S(1)}, f16[2,64,1500]{2,1,0:T(8,128)(2,1)S(1)}, u32[]{:S(2)}, u32[]{:S(2)}) collective-permute-start(f16[2,64,1500]{2,1,0:T(8,128)(2,1)S(1)} %get-tuple-element.29), channel_id=1, source_target_pairs={{0,16},{16,0},{32,48},{48,32},{64,80},{80,64},{96,112},{112,96},{1... | collective-permute-start | bytes 1152008 | tf_op jit(solution)/shard_map/ppermute | solution.py:48
  57.1 21.3 %collective-permute-start.5 = (bf16[2,2,2,32,1500]{4,3,2,1,0:T(8,128)(2,1)S(1)}, bf16[2,2,2,32,1500]{4,3,2,1,0:T(8,128)(2,1)S(1)}, u32[]{:S(2)}, u32[]{:S(2)}) collective-permute-start(bf16[2,2,2,32,1500]{4,3,2,1,0:T(8,128)(2,1)S(1)} %pad_maximum_fusion.2.near), channel_id=1, source_target_pairs={{0,32},{1,97},{2,34},{3,99},{4,36},{5,101},{6,38},{7,103},{8,40},{... | collective-permute-start | bytes 2304008 | tf_op jit(solution)/shard_map/ppermute | solution.py:48
  57.2 24.8 %slice-start.5 = ((s8[9216000]{0:T(1024)(128)(4,1)}), s8[827392]{0:T(1024)(128)(4,1)S(1)}, s32[]{:S(2)}) async-start(s8[9216000]{0:T(1024)(128)(4,1)} %bitcast.114), calls=%async_computation.5 | async-start | bytes 1654784
  62.1 11.4 %collective-permute-start.18 = (f16[2,64,1500]{2,1,0:T(8,128)(2,1)S(1)}, f16[2,64,1500]{2,1,0:T(8,128)(2,1)S(1)}, u32[]{:S(2)}, u32[]{:S(2)}) collective-permute-start(f16[2,64,1500]{2,1,0:T(8,128)(2,1)S(1)} %get-tuple-element.33), channel_id=1, source_target_pairs={{0,16},{16,0},{32,48},{48,32},{64,80},{80,64},{96,112},{112,96},{1... | collective-permute-start | bytes 1152008 | tf_op jit(solution)/shard_map/ppermute | solution.py:48
  73.6 1.5 collective-permute-start.19
  73.7 16.4 %collective-permute-start.14 = (bf16[2,32,1500]{2,1,0:T(8,128)(2,1)S(1)}, bf16[2,32,1500]{2,1,0:T(8,128)(2,1)S(1)}, u32[]{:S(2)}, u32[]{:S(2)}) collective-permute-start(bf16[2,32,1500]{2,1,0:T(8,128)(2,1)S(1)} %get-tuple-element.54), channel_id=1, source_target_pairs={{0,1},{1,0},{2,3},{3,2},{4,5},{5,4},{6,7},{7,6},{8,9},{9,8},{10,11... | collective-permute-start | bytes 576008 | tf_op jit(solution)/shard_map/ppermute | solution.py:48
  75.2 14.7 %collective-permute-start.20 = (bf16[2,2,32,1500]{3,2,1,0:T(8,128)(2,1)S(1)}, bf16[2,2,32,1500]{3,2,1,0:T(8,128)(2,1)S(1)}, u32[]{:S(2)}, u32[]{:S(2)}) collective-permute-start(bf16[2,2,32,1500]{3,2,1,0:T(8,128)(2,1)S(1)} %pad_maximum_fusion.11), channel_id=1, source_target_pairs={{0,96},{1,33},{2,98},{3,35},{4,100},{5,37},{6,102},{7,39},{8,104},... | collective-permute-start | bytes 1152008 | tf_op jit(solution)/shard_map/ppermute | solution.py:48
  78.4 3.6 %copy-start.2 = (bf16[1500,3000]{0,1:T(8,128)(2,1)}, bf16[1500,3000]{0,1:T(8,128)(2,1)S(1)}, u32[]{:S(2)}) copy-start(bf16[1500,3000]{0,1:T(8,128)(2,1)S(1)} %collective-permute-done.6) | copy-start | bytes 27000004
  90.0 15.4 %collective-permute-start.21 = (bf16[2,2,2,32,1500]{4,3,2,1,0:T(8,128)(2,1)S(1)}, bf16[2,2,2,32,1500]{4,3,2,1,0:T(8,128)(2,1)S(1)}, u32[]{:S(2)}, u32[]{:S(2)}) collective-permute-start(bf16[2,2,2,32,1500]{4,3,2,1,0:T(8,128)(2,1)S(1)} %pad_maximum_fusion.8.near), channel_id=1, source_target_pairs={{0,32},{1,97},{2,34},{3,99},{4,36},{5,101},{6,38},{7,103},{8,40},{... | collective-permute-start | bytes 2304008 | tf_op jit(solution)/shard_map/ppermute | solution.py:48
  90.2 13.3 %collective-permute-start.15 = (bf16[2,2,32,1500]{3,2,1,0:T(8,128)(2,1)S(1)}, bf16[2,2,32,1500]{3,2,1,0:T(8,128)(2,1)S(1)}, u32[]{:S(2)}, u32[]{:S(2)}) collective-permute-start(bf16[2,2,32,1500]{3,2,1,0:T(8,128)(2,1)S(1)} %copy.11), channel_id=1, source_target_pairs={{0,96},{1,33},{2,98},{3,35},{4,100},{5,37},{6,102},{7,39},{8,104},... | collective-permute-start | bytes 1152008 | tf_op jit(solution)/shard_map/ppermute | solution.py:48
  90.3 24.9 %collective-permute-start.7 = (bf16[1,2,64,3000]{3,2,1,0:T(8,128)(2,1)S(1)}, bf16[1,2,64,3000]{3,2,1,0:T(8,128)(2,1)S(1)}, u32[]{:S(2)}, u32[]{:S(2)}) collective-permute-start(bf16[1,2,64,3000]{3,2,1,0:T(8,128)(2,1)S(1)} %get-tuple-element.18), channel_id=1, source_target_pairs={{0,2},{1,7},{2,0},{3,5},{4,6},{5,3},{6,4},{7,1},{8,10},{9,15},{10,... | collective-permute-start | bytes 2304008 | tf_op jit(solution)/shard_map/ppermute | solution.py:48
  103.6 14.5 %collective-permute-start.16 = (bf16[2,2,2,32,1500]{4,3,2,1,0:T(8,128)(2,1)S(1)}, bf16[2,2,2,32,1500]{4,3,2,1,0:T(8,128)(2,1)S(1)}, u32[]{:S(2)}, u32[]{:S(2)}) collective-permute-start(bf16[2,2,2,32,1500]{4,3,2,1,0:T(8,128)(2,1)S(1)} %pad_maximum_fusion.7.near), channel_id=1, source_target_pairs={{0,32},{1,97},{2,34},{3,99},{4,36},{5,101},{6,38},{7,103},{8,40},{... | collective-permute-start | bytes 2304008 | tf_op jit(solution)/shard_map/ppermute | solution.py:48
  113.2 16.4 %collective-permute-start.22 = (bf16[1,2,64,3000]{3,2,1,0:T(8,128)(2,1)S(1)}, bf16[1,2,64,3000]{3,2,1,0:T(8,128)(2,1)S(1)}, u32[]{:S(2)}, u32[]{:S(2)}) collective-permute-start(bf16[1,2,64,3000]{3,2,1,0:T(8,128)(2,1)S(1)} %get-tuple-element.26), channel_id=1, source_target_pairs={{0,2},{1,7},{2,0},{3,5},{4,6},{5,3},{6,4},{7,1},{8,10},{9,15},{10,... | collective-permute-start | bytes 2304008 | tf_op jit(solution)/shard_map/ppermute | solution.py:48
  115.5 13.3 %collective-permute-start.8 = (bf16[1,64,3000]{2,1,0:T(8,128)(2,1)S(1)}, bf16[1,64,3000]{2,1,0:T(8,128)(2,1)S(1)}, u32[]{:S(2)}, u32[]{:S(2)}) collective-permute-start(bf16[1,64,3000]{2,1,0:T(8,128)(2,1)S(1)} %fusion.80), channel_id=1, source_target_pairs={{0,6},{1,3},{2,4},{3,1},{4,2},{5,7},{6,0},{7,5},{8,14},{9,11},{10,... | collective-permute-start | bytes 1152008 | tf_op jit(solution)/shard_map/ppermute | solution.py:48
  126.0 16.3 %collective-permute-start.23 = (bf16[1,2,64,3000]{3,2,1,0:T(8,128)(2,1)S(1)}, bf16[1,2,64,3000]{3,2,1,0:T(8,128)(2,1)S(1)}, u32[]{:S(2)}, u32[]{:S(2)}) collective-permute-start(bf16[1,2,64,3000]{3,2,1,0:T(8,128)(2,1)S(1)} %get-tuple-element.28), channel_id=1, source_target_pairs={{0,2},{1,7},{2,0},{3,5},{4,6},{5,3},{6,4},{7,1},{8,10},{9,15},{10,... | collective-permute-start | bytes 2304008 | tf_op jit(solution)/shard_map/ppermute | solution.py:48
  129.0 29.2 %collective-permute-start.9 = (bf16[32,3000]{1,0:T(8,128)(2,1)S(1)}, bf16[32,3000]{1,0:T(8,128)(2,1)S(1)}, u32[]{:S(2)}, u32[]{:S(2)}) collective-permute-start(bf16[32,3000]{1,0:T(8,128)(2,1)S(1)} %fusion.107), channel_id=1, source_target_pairs={{0,8},{1,9},{2,10},{3,11},{4,12},{5,13},{6,14},{7,15},{8,0},{9,1},... | collective-permute-start | bytes 576008 | tf_op jit(solution)/shard_map/ppermute | solution.py:48
  129.9 14.4 %collective-permute-start.26 = (bf16[1,64,3000]{2,1,0:T(8,128)(2,1)S(1)}, bf16[1,64,3000]{2,1,0:T(8,128)(2,1)S(1)}, u32[]{:S(2)}, u32[]{:S(2)}) collective-permute-start(bf16[1,64,3000]{2,1,0:T(8,128)(2,1)S(1)} %fusion.84), channel_id=1, source_target_pairs={{0,6},{1,3},{2,4},{3,1},{4,2},{5,7},{6,0},{7,5},{8,14},{9,11},{10,... | collective-permute-start | bytes 1152008 | tf_op jit(solution)/shard_map/ppermute | solution.py:48
  142.6 9.1 %collective-permute-start.24 = (bf16[1,64,3000]{2,1,0:T(8,128)(2,1)S(1)}, bf16[1,64,3000]{2,1,0:T(8,128)(2,1)S(1)}, u32[]{:S(2)}, u32[]{:S(2)}) collective-permute-start(bf16[1,64,3000]{2,1,0:T(8,128)(2,1)S(1)} %fusion.83), channel_id=1, source_target_pairs={{0,6},{1,3},{2,4},{3,1},{4,2},{5,7},{6,0},{7,5},{8,14},{9,11},{10,... | collective-permute-start | bytes 1152008 | tf_op jit(solution)/shard_map/ppermute | solution.py:48
  144.4 8.1 %collective-permute-start.27 = (bf16[32,3000]{1,0:T(8,128)(2,1)S(1)}, bf16[32,3000]{1,0:T(8,128)(2,1)S(1)}, u32[]{:S(2)}, u32[]{:S(2)}) collective-permute-start(bf16[32,3000]{1,0:T(8,128)(2,1)S(1)} %fusion.109), channel_id=1, source_target_pairs={{0,8},{1,9},{2,10},{3,11},{4,12},{5,13},{6,14},{7,15},{8,0},{9,1},... | collective-permute-start | bytes 576008 | tf_op jit(solution)/shard_map/ppermute | solution.py:48
  151.8 5.7 %collective-permute-start.25 = (bf16[32,3000]{1,0:T(8,128)(2,1)S(1)}, bf16[32,3000]{1,0:T(8,128)(2,1)S(1)}, u32[]{:S(2)}, u32[]{:S(2)}) collective-permute-start(bf16[32,3000]{1,0:T(8,128)(2,1)S(1)} %fusion.108), channel_id=1, source_target_pairs={{0,8},{1,9},{2,10},{3,11},{4,12},{5,13},{6,14},{7,15},{8,0},{9,1},... | collective-permute-start | bytes 576008 | tf_op jit(solution)/shard_map/ppermute | solution.py:48
  157.6 2.3 %copy-start.1 = (bf16[1000,768]{1,0:T(8,128)(2,1)S(1)}, bf16[1000,768]{1,0:T(8,128)(2,1)}, u32[]{:S(2)}) copy-start(bf16[1000,768]{1,0:T(8,128)(2,1)} %param.4) | copy-start | bytes 4608004
